TPU v7x, 256 devices: a whole 4x4x8 slice. The times are simulated.
256 devices in a mesh: leaf: 64 (over z, y, core), level: 4 (over x).
Axes of the slice: x: 4, y: 4, z: 8, core: 2. Of those that a mesh axis runs over, the one named last changes fastest.
Arguments:
- vectors: bfloat16 [2048, 32, 128], P('leaf'), may hold values from -6 to 6
- leaf_basis: bfloat16 [2048, 32, 128], P('leaf'), may hold values from -0.5 to 0.5
- transfer: bfloat16 [2048, 32, 32], P('leaf'), may hold values from -0.1875 to 0.1875
- nearfield_source_leaf: int32 [2048, 16], P('leaf', 'level'), may hold values from 0 to 2047, as said below
- near_count: int32 [2048], P('leaf'), may hold values from 1 to 16
- nearfield_block_matrix: bfloat16 [2048, 16, 128, 128], P('leaf', 'level'), may hold values from -0.25 to 0.25
- far_source: int32 [2048, 16], P('leaf', 'level'), may hold values from 0 to 2047, as said below
- far_count: int32 [2048], P('leaf'), may hold values from 1 to 16
- far_block: bfloat16 [2048, 16, 1024], P('leaf', 'level'), may hold values from -0.75 to 0.75
- top_source: int32 [64, 16], P('leaf', 'level'), may hold values from 0 to 63
- top_count: int32 [64], P('leaf'), may hold values from 1 to 16
- top_block: bfloat16 [64, 16, 1024], P('leaf', 'level'), may hold values from -1.5 to 1.5
Outputs:
- product: bfloat16 [2048, 32, 128], P('leaf', 'level')
Inputs may be any that keep to these rules, and one draw needn't show every extreme that they name: `nearfield_source_leaf`: each near-field source leaf lies within 32 leaves of its target leaf's index. `far_source`: each coupling source leaf lies within 32 leaves of its target leaf's index.
All inputs are finite; a program needn't handle non-finite values.
Results may differ from a plain program's by a relative error of at most 0.0036.
Values may be sent and summed in bfloat16 or wider, within the bound.
No kernel may reach another device: no remote copies, remote signals or barrier semaphores. Data moves between devices by JAX's collectives and lax.ppermute only.
A program may use at most 64 MiB of HBM per device.

v0:
```python
import jax
import jax.numpy as jnp
from jax import lax
from jax.sharding import PartitionSpec as P


def padded(value, sides, width):
    for axis, dim in sides:
        devices, length = (lax.axis_size(axis), value.shape[dim])
        up = [(i, (i + 1) % devices) for i in range(devices - 1)]
        down = [(j, i) for i, j in up]
        last = lax.slice_in_dim(value, length - width, length, axis=dim)
        initial = lax.slice_in_dim(value, 0, width, axis=dim)
        before = lax.ppermute(last, axis, up)
        after = lax.ppermute(initial, axis, down)
        value = jnp.concatenate([before, value, after], axis=dim)
    return value


def per_device(
    vectors,
    leaf_basis,
    transfer,
    nearfield_source_leaf,
    near_count,
    nearfield_block_matrix,
    far_source,
    far_count,
    far_block,
    top_source,
    top_count,
    top_block,
):
    leaves = vectors.shape[0]
    columns = vectors.shape[1]
    points = vectors.shape[2]
    ranks = leaf_basis.shape[1]
    level_pos = lax.axis_index("level")
    first_leaf = lax.axis_index("leaf") * leaves
    coefficients = jnp.einsum(
        "nrp,nkp->nkr", vectors, leaf_basis, preferred_element_type=jnp.float32
    ).astype(jnp.bfloat16)
    root_coef = jnp.einsum(
        "nab,nbr->ar", transfer, coefficients, preferred_element_type=jnp.float32
    ).astype(jnp.bfloat16)
    every_root_cluster = lax.all_gather(root_coef[None], "leaf", axis=0, tiled=True)
    packed_rows = ranks * columns // points
    packed = jnp.concatenate([vectors, coefficients.reshape(leaves, packed_rows, points)], axis=1)
    widened = padded(packed, (("leaf", 0),), leaves)
    near_rows = widened[:, :columns]
    coef_rows = widened[:, columns:].reshape(3 * leaves, ranks, columns)
    near_slots = nearfield_source_leaf.shape[1]
    near_active = (level_pos * near_slots + jnp.arange(near_slots, dtype=jnp.int32))[
        None, :
    ] < near_count[:, None]
    near_local = nearfield_source_leaf - first_leaf + leaves
    near_gathered = near_rows[near_local] * near_active[:, :, None, None].astype(jnp.bfloat16)
    near_sum = jnp.einsum(
        "nsrq,nspq->nrp", near_gathered, nearfield_block_matrix, preferred_element_type=jnp.float32
    )
    far_slots = far_source.shape[1]
    far_active = (level_pos * far_slots + jnp.arange(far_slots, dtype=jnp.int32))[
        None, :
    ] < far_count[:, None]
    far_local = far_source - first_leaf + leaves
    far_gathered = coef_rows[far_local] * far_active[:, :, None, None].astype(jnp.bfloat16)
    far_blocks = far_block.reshape(leaves, far_slots, ranks, ranks)
    far_sum = jnp.einsum(
        "nsab,nsbr->nar", far_blocks, far_gathered, preferred_element_type=jnp.float32
    )
    upper_level_slots = top_source.shape[1]
    top_active = (
        level_pos * upper_level_slots + jnp.arange(upper_level_slots, dtype=jnp.int32)
        < top_count[0]
    )
    upper_collected = every_root_cluster[top_source[0]] * top_active[:, None, None].astype(
        jnp.bfloat16
    )
    upper_level_blocks = top_block[0].reshape(upper_level_slots, ranks, ranks)
    top_sum = jnp.einsum(
        "djm,dmp->jp", upper_level_blocks, upper_collected, preferred_element_type=jnp.float32
    )
    lowered = jnp.einsum(
        "nab,ar->nbr", transfer.astype(jnp.float32), top_sum, precision=lax.Precision.HIGHEST
    )
    basis_wide = leaf_basis.astype(jnp.float32)
    near_total, down_total = (
        lax.psum_scatter(near_sum, "level", scatter_dimension=1, tiled=True),
        lax.psum_scatter(far_sum + lowered, "level", scatter_dimension=2, tiled=True),
    )
    result = near_total + jnp.einsum(
        "nkr,nkp->nrp", down_total, basis_wide, precision=lax.Precision.HIGHEST
    )
    return result.astype(jnp.bfloat16)


def solution(mesh):
    placed = (
        P("leaf", None, None),
        P("leaf", None, None),
        P("leaf", None, None),
        P("leaf", "level"),
        P("leaf"),
        P("leaf", "level", None, None),
        P("leaf", "level"),
        P("leaf"),
        P("leaf", "level", None),
        P("leaf", "level"),
        P("leaf"),
        P("leaf", "level", None),
    )
    return jax.shard_map(
        per_device, mesh=mesh, in_specs=placed, out_specs=P("leaf", "level", None), check_vma=False
    )
```

profile of v0, /device:TPU:1, one launch (start us, length us, event | category | flops | bytes accessed | tf_op | source)
XLA Modules:
  0.0 141.2 jit_solution(1049229063599630521)
XLA Ops:
  6.5 1.0 constant_dynamic-update-slice_fusion.1
  7.6 1.2 convolution_convert_fusion
  9.0 5.1 %collective-permute-start.1 = (bf16[32,40,128]{2,1,0:T(8,128)(2,1)S(1)}, bf16[32,40,128]{2,1,0:T(8,128)(2,1)S(1)}, u32[]{:S(2)}, u32[]{:S(2)}) collective-permute-start(bf16[32,40,128]{2,1,0:T(8,128)(2,1)S(1)} %constant_dynamic-update-slice_fusion), channel_id=1, source_target_pairs={{4,0},{8,4},{12,8},{16,12},{20,16},{24,20},{28,24},{32,28},{36,32}... | collective-permute-start | bytes 983048 | tf_op jit(solution)/shard_map/ppermute | solution.py:15
  14.1 1.9 %collective-permute-start = (bf16[32,40,128]{2,1,0:T(8,128)(2,1)S(1)}, bf16[32,40,128]{2,1,0:T(8,128)(2,1)S(1)}, u32[]{:S(2)}, u32[]{:S(2)}) collective-permute-start(bf16[32,40,128]{2,1,0:T(8,128)(2,1)S(1)} %constant_dynamic-update-slice_fusion), channel_id=1, source_target_pairs={{0,4},{4,8},{8,12},{12,16},{16,20},{20,24},{24,28},{28,32},{32,36}... | collective-permute-start | bytes 983048 | tf_op jit(solution)/shard_map/ppermute | solution.py:14
  16.7 0.7 fusion.11
  17.4 0.7 compare_convert_fusion.1
  18.1 0.7 copy.48
  18.9 0.7 compare_select_fusion
  20.1 0.8 reshape_squeeze.3
  20.8 1.2 fusion.3
  22.1 53.8 %all-gather = bf16[2048,32]{1,0:T(8,128)(2,1)S(1)} all-gather(bf16[32,32]{1,0:T(8,128)(2,1)S(1)} %copy.51), channel_id=2, replica_groups=mesh['leaf'=64,'level'=4] {'leaf'}, dimensions={0}, use_global_device_ids=true | all-gather | bytes 133120 | tf_op jit(solution)/shard_map/all_gather | solution.py:46
  75.9 1.8 %reshape.110 = bf16[32,4,32,32]{3,2,1,0:T(8,128)(2,1)S(1)} reshape(bf16[32,4,1024]{2,1,0:T(4,128)(2,1)} %param.20) | data formatting | bytes 524288 | tf_op jit(solution)/shard_map/reshape | solution.py:67
  77.7 0.6 gather_fusion.2
  78.3 0.9 fusion.8
  79.4 0.2 copy.45
  79.6 1.2 copy.47
  80.8 1.7 %gather_fusion.1 = bf16[128,32,32]{2,1,0:T(8,128)(2,1)} fusion(bf16[96,32,32]{2,1,0:T(8,128)(2,1)S(1)} %copy.47, s32[1024]{0:T(1024)S(1)} %pad_clamp_fusion.1), kind=kCustom, calls=%fused_computation.1 | custom fusion | bytes 524800 | tf_op jit(solution)/shard_map/gather | solution.py:66
  82.5 1.9 %convolution_bitcast_fusion = f32[32,32,32]{1,2,0:T(8,128)S(1)} fusion(bf16[32,4,32,32]{3,2,1,0:T(8,128)(2,1)S(1)} %reshape.110, bf16[32,4,32,32]{3,2,1,0:T(8,128)(2,1)} %bitcast.43, bf16[32,4]{1,0:T(8,128)(2,1)} %copy.48), kind=kOutput, calls=%fused_computation.3 | convolution fusion | flops 8519680 | bytes 655616 | tf_op jit(solution)/shard_map/nsab,nsbr->nar/dot_general | solution.py:68
  84.4 2.1 %fusion = f32[32,32,32]{1,2,0:T(8,128)} fusion(f32[32,32,32]{1,2,0:T(8,128)S(1)} %convolution_bitcast_fusion, f32[32,32,1]{1,0,2:T(8,128)S(1)} %copy-done.1, bf16[32,32,32]{2,1,0:T(8,128)(2,1)} %param.14), kind=kOutput, calls=%fused_computation.5 | convolution fusion | flops 12615680 | bytes 331776 | tf_op jit(solution)/shard_map/nab,ar->nbr/dot_general | solution.py:83
  86.5 0.8 gather_fusion
  87.3 4.5 %convolution_bitcast_fusion.2 = f32[32,32,128]{2,1,0:T(8,128)} fusion(bf16[32,4,128,128]{3,2,1,0:T(8,128)(2,1)} %param.17, bf16[32,4,32,128]{3,2,1,0:T(8,128)(2,1)S(1)} %bitcast.42, bf16[32,4]{1,0:T(8,128)(2,1)S(1)} %copy.44), kind=kOutput, calls=%fused_computation.6 | convolution fusion | flops 134742016 | bytes 5767424 | tf_op jit(solution)/shard_map/nsrq,nspq->nrp/dot_general | solution.py:58
  91.8 14.3 %reduce-scatter.5.cloned.1.call-done = f32[32,32,8]{1,2,0:T(8,128)} async-done(((f32[32,32,32]{1,2,0:T(8,128)}), f32[32,32,8]{1,2,0:T(8,128)}) %reduce-scatter.5.cloned.1.call-update) | async-done | bytes 32784 | tf_op jit(solution)/shard_map/reduce_scatter | solution.py:89
  106.2 26.3 %reduce-scatter.3.cloned.1.call-done = f32[32,8,128]{2,1,0:T(8,128)} async-done(((f32[32,32,128]{2,1,0:T(8,128)}), f32[32,8,128]{2,1,0:T(8,128)}) %reduce-scatter.3.cloned.1.call-update) | async-done | bytes 131088 | tf_op jit(solution)/shard_map/reduce_scatter | solution.py:88
  132.5 1.9 %fusion.1 = bf16[32,8,128]{2,1,0:T(8,128)(2,1)} fusion(f32[32,8,128]{2,1,0:T(8,128)} %reduce-scatter.3.cloned.1.call-done, f32[32,32,8]{1,2,0:T(8,128)} %reduce-scatter.5.cloned.1.call-done, bf16[32,32,128]{2,1,0:T(8,128)(2,1)S(1)} %copy-done), kind=kOutput, calls=%fused_computation.9 | convolution fusion | flops 12648448 | bytes 491520 | tf_op jit(solution)/shard_map/nkr,nkp->nrp/dot_general | solution.py:91
  (26 shorter events, 1.1 us)
Async XLA Ops:
  6.5 1.0 copy-start
  6.5 99.6 %reduce-scatter.5.cloned.1.call-start = ((), (), s32[]{:S(2)}) async-start(), calls=%async_computation.3 | async-start | bytes 655360 | tf_op jit(solution)/shard_map/reduce_scatter | solution.py:89
  9.0 70.2 %collective-permute-start.1 = (bf16[32,40,128]{2,1,0:T(8,128)(2,1)S(1)}, bf16[32,40,128]{2,1,0:T(8,128)(2,1)S(1)}, u32[]{:S(2)}, u32[]{:S(2)}) collective-permute-start(bf16[32,40,128]{2,1,0:T(8,128)(2,1)S(1)} %constant_dynamic-update-slice_fusion), channel_id=1, source_target_pairs={{4,0},{8,4},{12,8},{16,12},{20,16},{24,20},{28,24},{32,28},{36,32}... | collective-permute-start | bytes 983048 | tf_op jit(solution)/shard_map/ppermute | solution.py:15
  14.1 65.0 %collective-permute-start = (bf16[32,40,128]{2,1,0:T(8,128)(2,1)S(1)}, bf16[32,40,128]{2,1,0:T(8,128)(2,1)S(1)}, u32[]{:S(2)}, u32[]{:S(2)}) collective-permute-start(bf16[32,40,128]{2,1,0:T(8,128)(2,1)S(1)} %constant_dynamic-update-slice_fusion), channel_id=1, source_target_pairs={{0,4},{4,8},{8,12},{12,16},{16,20},{20,24},{24,28},{28,32},{32,36}... | collective-permute-start | bytes 983048 | tf_op jit(solution)/shard_map/ppermute | solution.py:14
  79.4 5.0 %copy-start.1 = (f32[32,32,1]{1,0,2:T(8,128)S(1)}, f32[32,32,1]{1,0,2:T(8,128)}, u32[]{:S(2)}) copy-start(f32[32,32,1]{1,0,2:T(8,128)} %fusion.8) | copy-start | bytes 12292
  86.5 46.0 %reduce-scatter.3.cloned.1.call-start = ((), (), s32[]{:S(2)}) async-start(), calls=%async_computation.2 | async-start | bytes 655360 | tf_op jit(solution)/shard_map/reduce_scatter | solution.py:88
Sparse Core Ops, SparseCore 0:
  86.6 19.5 reduce-scatter.4
  108.7 23.7 reduce-scatter.2
where the time goes:
time: 142 us; the launch traced here: 141 us
  blocking collectives  53.8 us (38%)
  waiting for transfers between devices  40.7 us (29%)
  between operations  14.2 us (10%)
  matrix products  13.6 us (10%)
  local copies, waits for them, and re-layouts  9.56 us (7%)
  starting transfers between devices  7.11 us (5%)
  other arithmetic  2.26 us (2%)
    all_gather x1, blocking collectives, per_device(): lax.all_gather(root_coef[None], 'leaf', axis=0, tiled=True)  53.8 us
    reduce_scatter x1, waiting for transfers between devices, per_device(): lax.psum_scatter(near_sum, 'level', scatter_dimension=1, tiled=True)  26.3 us
    reduce_scatter x1, waiting for transfers between devices, per_device(): lax.psum_scatter(far_sum + lowered, 'level', scatter_dimension=2, tiled=T...  14.3 us
    ppermute x1, starting transfers between devices, padded(): after = lax.ppermute(initial, axis, down)  5.15 us
    dot_general x1, matrix products, per_device(): jnp.einsum('nsrq,nspq->nrp', near_gathered, nearfield_block_matrix, prefe...  4.51 us
  transfers between devices with their start and end apart: 4, of which 2 were waited for; matrix products, arithmetic and copies ran while one was open for 10% of the time, Pallas kernels for 0%

commit v1 on v0

v1 whole, which is shorter than its diff:
```python
import jax
import jax.numpy as jnp
from jax import lax
from jax.experimental import pallas as pl
from jax.experimental.pallas import tpu as pltpu
from jax.sharding import PartitionSpec as P

BF = jnp.bfloat16
F32 = jnp.float32
LEAVES = 32
GROUP = 4
PACKED = LEAVES + LEAVES // GROUP
ROWS = 8
STEPS = 4
PER_STEP = LEAVES // STEPS
NONE = 3 * LEAVES


def dot_nt(a, b):
    return lax.dot_general(a, b, (((1,), (1,)), ((), ())), preferred_element_type=F32)


def dot_nn(a, b):
    return lax.dot_general(a, b, (((1,), (0,)), ((), ())), preferred_element_type=F32)


def two_terms(value):
    high = value.astype(BF)
    return high, (value - high.astype(F32)).astype(BF)


def coef_kernel(level, vectors, basis, transfer, packed, root, wide):
    packed[0:LEAVES] = vectors[...]
    total = jnp.zeros((32, 32), F32)
    for g in range(LEAVES // GROUP):
        pieces = []
        for m in range(GROUP):
            i = g * GROUP + m
            c = dot_nt(vectors[i], basis[i]).astype(BF)
            total = total + dot_nt(c, transfer[i])
            pieces.append(c)
        packed[LEAVES + g] = jnp.concatenate(pieces, axis=1)
    wide[...] = jnp.concatenate([total] * GROUP, axis=1)
    first = pl.multiple_of(level[0] * ROWS, ROWS)
    root[...] = wide[pl.ds(first, ROWS), :].astype(BF)


def near_far_kernel(
    level, near_at, far_at, top_at, own, before, after, blocks, far, basis, kept, out1, out2, out3, vtab, ctab, prod
):
    step = pl.program_id(0)

    @pl.when(step == 0)
    def _():
        for n, part in enumerate((before, own, after)):
            vtab[n * LEAVES : (n + 1) * LEAVES] = part[0:LEAVES]
            lane = lax.broadcasted_iota(jnp.int32, (32, 128), 1) // 32
            for g in range(LEAVES // GROUP):
                tile = part[LEAVES + g].astype(F32)
                turned = [tile] + [pltpu.roll(tile, 32 * k, 1) for k in range(1, GROUP)]
                for m in range(GROUP):
                    v = turned[(0 - m) % GROUP]
                    for k in range(1, GROUP):
                        v = jnp.where(lane == k, turned[(k - m) % GROUP], v)
                    ctab[n * LEAVES + g * GROUP + m] = v.astype(BF)
        vtab[NONE] = jnp.zeros((32, 128), BF)
        ctab[NONE] = jnp.zeros((32, 128), BF)
        top = far[LEAVES]
        row = lax.broadcasted_iota(jnp.int32, (16, 128), 0)
        names = jnp.full((16, 128), -1, jnp.int32)
        for s in range(4):
            names = jnp.where(row == s, top_at[s], names)
        for out in (out1, out2, out3):
            out[LEAVES // 2 + 2] = names.astype(F32).astype(BF)
            out[LEAVES // 2] = top[0:16]
            out[LEAVES // 2 + 1] = top[16:32]

    me = level[0]
    lane = lax.broadcasted_iota(jnp.int32, (32, 128), 1) // 32
    for j in range(PER_STEP):
        i = step * PER_STEP + j
        value = jnp.zeros((32, 128), F32)
        for s in range(4):
            value = value + dot_nt(vtab[near_at[i * 4 + s]], blocks[j, s])
        c = ctab[far_at[i * 4]]
        for s in range(1, 4):
            c = jnp.where(lane == s, ctab[far_at[i * 4 + s]], c)
        down = dot_nt(c, far[i])
        high, low = two_terms(down)
        b = basis[i]
        value = value + dot_nn(high, b) + dot_nn(low, b)
        prod[j] = value
    for h in range(PER_STEP // 2):
        pair = step * (PER_STEP // 2) + h

        def rows(k):
            at = pl.multiple_of(lax.rem(me + k, 4) * ROWS, ROWS)
            return jnp.concatenate([prod[2 * h, pl.ds(at, ROWS), :], prod[2 * h + 1, pl.ds(at, ROWS), :]], axis=0)

        kept[pair] = rows(0)
        for k, out in ((1, out1), (2, out2), (3, out3)):
            out[pair] = rows(k).astype(BF)


def top_operator_kernel(transfer, basis, operator):
    for i in range(LEAVES):
        high, low = two_terms(dot_nn(transfer[i], basis[i]))
        operator[0:32, i * 128 : (i + 1) * 128] = high
        operator[32:64, i * 128 : (i + 1) * 128] = low


def final_kernel(top_at, roots, far, operator, kept, got1, got2, got3, out):
    lane = lax.broadcasted_iota(jnp.int32, (ROWS, 128), 1) // 32
    total = jnp.zeros((ROWS, 32), F32)
    for k, got in enumerate((None, got1, got2, got3)):
        c = jnp.zeros((ROWS, 128), F32)
        for s in range(4):
            at = top_at[k * 4 + s]
            row = roots[jnp.maximum(at, 0)].astype(F32)
            c = jnp.where((lane == s) & (at >= 0), row, c)
        c = c.astype(BF)
        if got is None:
            total = total + dot_nt(c, far[0])
        else:
            total = total + dot_nt(c, jnp.concatenate([got[LEAVES // 2], got[LEAVES // 2 + 1]], axis=0))
    high, low = two_terms(total)
    lhs = jnp.concatenate([high, low], axis=1)
    for h in range(LEAVES // 2):
        value = kept[h] + got1[h].astype(F32) + got2[h].astype(F32) + got3[h].astype(F32)
        halves = []
        for n in range(2):
            w = operator[:, (2 * h + n) * 128 : (2 * h + n + 1) * 128]
            t = dot_nn(lhs, jnp.concatenate([w[0:32], w[0:32]], axis=0)) + dot_nn(high, w[32:64])
            halves.append(t)
        out[h] = (value + jnp.concatenate(halves, axis=0)).astype(BF)


def whole(shape):
    return pl.BlockSpec(shape, lambda *_: (0,) * len(shape))


SMEM = pl.BlockSpec(memory_space=pltpu.SMEM)


def per_device(
    vectors,
    leaf_basis,
    transfer,
    nearfield_source_leaf,
    near_count,
    nearfield_block_matrix,
    far_source,
    far_count,
    far_block,
    top_source,
    top_count,
    top_block,
):
    level = lax.axis_index("level")
    leaf = lax.axis_index("leaf")
    level_in = level.reshape(1).astype(jnp.int32)
    packed, root = pl.pallas_call(
        coef_kernel,
        out_shape=(
            jax.ShapeDtypeStruct((PACKED, 32, 128), BF),
            jax.ShapeDtypeStruct((ROWS, 128), BF),
        ),
        in_specs=[SMEM, whole((32, 32, 128)), whole((32, 32, 128)), whole((32, 32, 32))],
        out_specs=(whole((PACKED, 32, 128)), whole((ROWS, 128))),
        scratch_shapes=[pltpu.VMEM((32, 128), F32)],
        name="coefficients",
    )(level_in, vectors, leaf_basis, transfer)

    up = [(n, n + 1) for n in range(63)]
    down = [(n + 1, n) for n in range(63)]
    before = lax.ppermute(packed, "leaf", up)
    after = lax.ppermute(packed, "leaf", down)
    roots = lax.all_to_all(
        jnp.broadcast_to(root[None], (64, ROWS, 128)), "leaf", 0, 0, tiled=True
    )

    slot = level * 4 + jnp.arange(4, dtype=jnp.int32)
    shift = LEAVES - leaf * LEAVES
    near_at = jnp.where(slot[None] < near_count[:, None], nearfield_source_leaf + shift, NONE).reshape(-1)
    far_at = jnp.where(slot[None] < far_count[:, None], far_source + shift, NONE).reshape(-1)
    couplings = jnp.concatenate([far_block, top_block], axis=0)
    couplings = couplings.reshape(LEAVES + 1, 4, 32, 32).transpose(0, 2, 1, 3).reshape(LEAVES + 1, 32, 128)

    operator = pl.pallas_call(
        top_operator_kernel,
        out_shape=jax.ShapeDtypeStruct((64, LEAVES * 128), BF),
        in_specs=[whole((32, 32, 32)), whole((32, 32, 128))],
        out_specs=whole((64, LEAVES * 128)),
        name="top_operator",
    )(transfer, leaf_basis)

    parts = LEAVES // 2
    top_live = jnp.where(slot < top_count[0], top_source[0], -1)
    sent = jax.ShapeDtypeStruct((parts + 3, 16, 128), BF)
    kept, *outs = pl.pallas_call(
        near_far_kernel,
        grid=(STEPS,),
        out_shape=(jax.ShapeDtypeStruct((parts, 16, 128), F32), sent, sent, sent),
        in_specs=[
            SMEM,
            SMEM,
            SMEM,
            SMEM,
            whole((PACKED, 32, 128)),
            whole((PACKED, 32, 128)),
            whole((PACKED, 32, 128)),
            pl.BlockSpec((PER_STEP, 4, 128, 128), lambda n: (n, 0, 0, 0)),
            whole((LEAVES + 1, 32, 128)),
            whole((LEAVES, 32, 128)),
        ],
        out_specs=(whole((parts, 16, 128)),) + (whole((parts + 3, 16, 128)),) * 3,
        scratch_shapes=[
            pltpu.VMEM((NONE + 1, 32, 128), BF),
            pltpu.VMEM((NONE + 1, 32, 128), BF),
            pltpu.VMEM((PER_STEP, 32, 128), F32),
        ],
        name="near_far",
    )(level_in, near_at, far_at, top_live, packed, before, after, nearfield_block_matrix, couplings, leaf_basis)

    got = []
    for k, out in zip((1, 2, 3), outs):
        got.append(lax.ppermute(out, "level", [(n, (n + k) % 4) for n in range(4)]))

    top_at = jnp.concatenate(
        [top_live] + [part[parts + 2, 0:4, 0].astype(jnp.int32) for part in got]
    )
    result = pl.pallas_call(
        final_kernel,
        out_shape=jax.ShapeDtypeStruct((parts, 16, 128), BF),
        grid=(1,),
        in_specs=[
            SMEM,
            whole((64, ROWS, 128)),
            pl.BlockSpec((1, 32, 128), lambda n: (LEAVES, 0, 0)),
            whole((64, LEAVES * 128)),
            whole((parts, 16, 128)),
            whole((parts + 3, 16, 128)),
            whole((parts + 3, 16, 128)),
            whole((parts + 3, 16, 128)),
        ],
        out_specs=whole((parts, 16, 128)),
        name="final",
    )(top_at, roots, couplings, operator, kept, *got)
    return result.reshape(LEAVES, ROWS, 128)


def solution(mesh):
    placed = (
        P("leaf", None, None),
        P("leaf", None, None),
        P("leaf", None, None),
        P("leaf", "level"),
        P("leaf"),
        P("leaf", "level", None, None),
        P("leaf", "level"),
        P("leaf"),
        P("leaf", "level", None),
        P("leaf", "level"),
        P("leaf"),
        P("leaf", "level", None),
    )
    return jax.shard_map(
        per_device, mesh=mesh, in_specs=placed, out_specs=P("leaf", "level", None), check_vma=False
    )
```

time: 142 us -> 56.1 us (0.40)
  blocking collectives: 53.8 us -> 0 us
  waiting for transfers between devices: 40.7 us -> 7 us
  starting transfers between devices: 7.11 us -> 23.4 us
  Pallas kernels: 0 us -> 14.5 us
  matrix products: 13.6 us -> 0 us
  between operations: 14.2 us -> 0.75 us
  local copies, waits for them, and re-layouts: 9.56 us -> 6.71 us
    all_gather x1 -> x0, blocking collectives: 53.8 us -> none  [per_device(): lax.all_gather(root_coef[None], 'leaf', axis=0, tiled=True)]
    reduce_scatter x2 -> x0, waiting for transfers between devices: 40.6 us -> none  [the longest x1 26.3 us: per_device(): lax.psum_scatter(near_sum, 'level', scatter_dimension=1, tiled=True)]
    pallas_call x0 -> x4, Pallas kernels: none -> 14.5 us  [the longest x1 7.56 us: per_device(): pl.pallas_call(near_far_kernel, grid=(STEPS,), out_shape=(jax.ShapeDtypeS...]
    dot_general x7 -> x0, matrix products: 13.6 us -> none  [the longest x1 4.51 us: per_device(): jnp.einsum('nsrq,nspq->nrp', near_gathered, nearfield_block_matrix, prefe...]
    all_to_all x0 -> x1, starting transfers between devices: none -> 13.2 us  [per_device(): lax.all_to_all(jnp.broadcast_to(root[None], (64, ROWS, 128)), 'leaf', 0,...]
    ppermute x2 -> x5, waiting for transfers between devices: 0.01 us -> 5.85 us  [the longest x3 5.85 us: per_device(): got.append(lax.ppermute(out, 'level', [(n, (n + k) % 4) for n in range(4)]))]
    ppermute x2 -> x5, starting transfers between devices: 7.07 us -> 10.2 us  [the longest x1 4.58 us: per_device(): before = lax.ppermute(packed, 'leaf', up)]
    gather x3 -> x0, local copies, waits for them, and re-layouts: 2.98 us -> none  [the longest x1 1.66 us: per_device(): coef_rows[far_local] * far_active[:, :, None, None].astype(jnp.bfloat16)]
  transfers between devices with their start and end apart: 4 -> 6, of which waited for: 2 -> 3; matrix products, arithmetic and copies ran while one was open for 10% -> 14% of each run, Pallas kernels for 0% -> 4%
where the time goes in v1:
time: 56.1 us; the launch traced here: 55.8 us
  starting transfers between devices  23.4 us (42%)
  Pallas kernels  14.5 us (26%)
  waiting for transfers between devices  7 us (12%)
  local copies, waits for them, and re-layouts  6.71 us (12%)
  other arithmetic  3.44 us (6%)
  between operations  0.75 us (1%)
    all_to_all x1, starting transfers between devices, per_device(): lax.all_to_all(jnp.broadcast_to(root[None], (64, ROWS, 128)), 'leaf', 0,...  13.2 us
    pallas_call x1, Pallas kernels, per_device(): pl.pallas_call(near_far_kernel, grid=(STEPS,), out_shape=(jax.ShapeDtypeS...  7.56 us
    ppermute x3, waiting for transfers between devices, per_device(): got.append(lax.ppermute(out, 'level', [(n, (n + k) % 4) for n in range(4)]))  5.85 us
    ppermute x1, starting transfers between devices, per_device(): before = lax.ppermute(packed, 'leaf', up)  4.58 us
    ppermute x3, starting transfers between devices, per_device(): got.append(lax.ppermute(out, 'level', [(n, (n + k) % 4) for n in range(4)]))  3.68 us
    pallas_call x1, Pallas kernels, per_device(): pl.pallas_call(final_kernel, out_shape=jax.ShapeDtypeStruct((parts, 16, 1...  2.46 us
    pallas_call x1, Pallas kernels, per_device(): pl.pallas_call(coef_kernel, out_shape=(jax.ShapeDtypeStruct((PACKED, 32,...  2.43 us
    unnamed x22, local copies, waits for them, and re-layouts  2.11 us
  transfers between devices with their start and end apart: 6, of which 3 were waited for; matrix products, arithmetic and copies ran while one was open for 14% of the time, Pallas kernels for 4%

profile of v1, /device:TPU:1, one launch (start us, length us, event | category | flops | bytes accessed | tf_op | source)
XLA Modules:
  0.0 55.8 jit_solution(16544801379283785390)
XLA Ops:
  0.0 2.4 %coefficients.1 = (bf16[40,32,128]{2,1,0:T(8,128)(2,1)}, bf16[8,128]{1,0:T(8,128)(2,1)}) custom-call(s32[1]{0:T(128)} %bitcast.2.level, bf16[32,32,128]{2,1,0:T(8,128)(2,1)} %vectors.1, bf16[32,32,128]{2,1,0:T(8,128)(2,1)} %basis.5, bf16[32,32,32]{2,1,0:T(8,128)(2,1)} %transfer.3), custom_call_target="tpu_custom_call" | custom-call | tf_op jit(solution)/shard_map/coefficients/pallas_call | solution.py:162
  2.4 4.6 %collective-permute-start = (bf16[40,32,128]{2,1,0:T(8,128)(2,1)}, bf16[40,32,128]{2,1,0:T(8,128)(2,1)S(1)}, u32[]{:S(2)}, u32[]{:S(2)}) collective-permute-start(bf16[40,32,128]{2,1,0:T(8,128)(2,1)} %get-tuple-element.11.own), channel_id=1, source_target_pairs={{0,4},{4,8},{8,12},{12,16},{16,20},{20,24},{24,28},{28,32},{32,36}... | collective-permute-start | bytes 983048 | tf_op jit(solution)/shard_map/ppermute | solution.py:176
  7.0 1.9 %collective-permute-start.1 = (bf16[40,32,128]{2,1,0:T(8,128)(2,1)}, bf16[40,32,128]{2,1,0:T(8,128)(2,1)S(1)}, u32[]{:S(2)}, u32[]{:S(2)}) collective-permute-start(bf16[40,32,128]{2,1,0:T(8,128)(2,1)} %get-tuple-element.11.own), channel_id=1, source_target_pairs={{4,0},{8,4},{12,8},{16,12},{20,16},{24,20},{28,24},{32,28},{36,32}... | collective-permute-start | bytes 983048 | tf_op jit(solution)/shard_map/ppermute | solution.py:177
  9.0 0.8 %add_select_fusion = (s32[32,4]{0,1:T(4,128)S(1)}, s32[32,4]{0,1:T(4,128)S(1)}) fusion(s32[32,4]{0,1:T(4,128)} %param.18, s32[32]{0:T(128)} %param.19, s32[]{:T(128)S(6)} %sub.3, s32[4]{0:T(128)S(1)} %iota_add_fusion, s32[32,4]{0,1:T(4,128)} %param.15, s32[32]{0:T(128)} %param.16), kind=kLoop, calls=%fused_computation.4 | loop fusion | flops 768 | bytes 2324 | tf_op jit(solution)/shard_map/jit(_where)/select_n | solution.py:185
  9.8 0.7 %reshape.32.near_at = s32[128]{0:T(128)} reshape(s32[32,4]{1,0:T(8,128)S(1)} %copy.16) | data formatting | bytes 1024 | tf_op jit(solution)/shard_map/reshape | solution.py:184
  10.6 0.7 %reshape.33.far_at = s32[128]{0:T(128)} reshape(s32[32,4]{1,0:T(8,128)S(1)} %copy.17) | data formatting | bytes 1024 | tf_op jit(solution)/shard_map/reshape | solution.py:185
  11.9 1.1 %pad_maximum_fusion = bf16[33,4,1024]{2,1,0:T(4,128)(2,1)S(1)} fusion(bf16[1,4,1024]{2,1,0:T(4,128)(2,1)} %param.23, bf16[32,4,1024]{2,1,0:T(4,128)(2,1)} %param.20), kind=kLoop, calls=%fused_computation | loop fusion | flops 135168 | bytes 540672 | tf_op jit(solution)/shard_map/concatenate | solution.py:186
  13.1 0.6 %reshape.34 = bf16[33,4,32,32]{3,2,1,0:T(8,128)(2,1)S(1)} reshape(bf16[33,4,1024]{2,1,0:T(4,128)(2,1)S(1)} %pad_maximum_fusion) | data formatting | bytes 540672 | tf_op jit(solution)/shard_map/reshape | solution.py:187
  14.3 1.3 %reshape.35.far = bf16[33,32,128]{2,1,0:T(8,128)(2,1)} reshape(bf16[33,32,4,32]{3,2,1,0:T(4,128)(2,1)S(1)} %copy.18) | data formatting | bytes 540672 | tf_op jit(solution)/shard_map/reshape | solution.py:187
  15.5 0.6 %compare_select_fusion.top_at = s32[4]{0:T(128)} fusion(s32[1,4]{1,0:T(1,128)S(1)} %copy-done.8, s32[]{:T(128)} %bitcast.6, s32[]{:T(128)S(6)} %mul.6), kind=kLoop, calls=%fused_computation.6 | loop fusion | flops 12 | bytes 40 | tf_op jit(solution)/shard_map/jit(_where)/select_n | solution.py:198
  16.1 0.7 %copy-done.1 = bf16[40,32,128]{2,1,0:T(8,128)(2,1)} copy-done((bf16[40,32,128]{2,1,0:T(8,128)(2,1)}, bf16[40,32,128]{2,1,0:T(8,128)(2,1)S(1)}, u32[]{:S(2)}) %copy-start.1) | copy-done | bytes 327704
  16.8 0.7 %copy-done.2 = bf16[40,32,128]{2,1,0:T(8,128)(2,1)} copy-done((bf16[40,32,128]{2,1,0:T(8,128)(2,1)}, bf16[40,32,128]{2,1,0:T(8,128)(2,1)S(1)}, u32[]{:S(2)}) %copy-start.2) | copy-done | bytes 327704
  17.6 7.6 %near_far.1 = (f32[16,16,128]{2,1,0:T(8,128)}, bf16[19,16,128]{2,1,0:T(8,128)(2,1)}, bf16[19,16,128]{2,1,0:T(8,128)(2,1)}, bf16[19,16,128]{2,1,0:T(8,128)(2,1)}) custom-call(s32[1]{0:T(128)} %bitcast.2.level, s32[128]{0:T(128)} %reshape.32.near_at, s32[128]{0:T(128)} %reshape.33.far_at, s32[4]{0:T(128)} %compare_select_fusion.top_at, ...), custom_call_target="tpu_custom_call" | custom-call | tf_op jit(solution)/shard_map/near_far/pallas_call | solution.py:200
  25.1 2.6 %collective-permute-start.4 = (bf16[19,16,128]{2,1,0:T(8,128)(2,1)}, bf16[19,16,128]{2,1,0:T(8,128)(2,1)S(1)}, u32[]{:S(2)}, u32[]{:S(2)}) collective-permute-start(bf16[19,16,128]{2,1,0:T(8,128)(2,1)} %get-tuple-element.14), channel_id=1, source_target_pairs={{0,3},{1,0},{2,1},{3,2},{4,7},{5,4},{6,5},{7,6},{8,11},{9,8},{10,9... | collective-permute-start | bytes 233480 | tf_op jit(solution)/shard_map/ppermute | solution.py:227
  27.7 0.7 %broadcast_in_dim.21 = bf16[64,8,128]{2,1,0:T(8,128)(2,1)} broadcast(bf16[8,128]{1,0:T(8,128)(2,1)S(1)} %copy-done.7), dimensions={1,2} | broadcast | bytes 133120 | tf_op jit(solution)/shard_map/broadcast_in_dim | solution.py:179
  28.4 13.2 %all-to-all-start = ((bf16[64,8,128]{2,1,0:T(8,128)(2,1)}), bf16[64,8,128]{2,1,0:T(8,128)(2,1)S(1)}, u32[]{:S(2)}, u32[]{:S(2)}) async-start(bf16[64,8,128]{2,1,0:T(8,128)(2,1)} %broadcast_in_dim.21), calls=%async_computation | async-start | bytes 262144 | tf_op jit(solution)/shard_map/all_to_all | solution.py:178
  41.5 2.1 %top_operator.1.operator = bf16[64,4096]{1,0:T(8,128)(2,1)} custom-call(bf16[32,32,32]{2,1,0:T(8,128)(2,1)} %transfer.3, bf16[32,32,128]{2,1,0:T(8,128)(2,1)} %basis.5), custom_call_target="tpu_custom_call" | custom-call | tf_op jit(solution)/shard_map/top_operator/pallas_call | solution.py:189
  44.1 0.6 %collective-permute-start.2 = (bf16[19,16,128]{2,1,0:T(8,128)(2,1)S(1)}, bf16[19,16,128]{2,1,0:T(8,128)(2,1)S(1)}, u32[]{:S(2)}, u32[]{:S(2)}) collective-permute-start(bf16[19,16,128]{2,1,0:T(8,128)(2,1)S(1)} %copy-done.9), channel_id=1, source_target_pairs={{0,1},{1,2},{2,3},{3,0},{4,5},{5,6},{6,7},{7,4},{8,9},{9,10},{10,1... | collective-permute-start | bytes 233480 | tf_op jit(solution)/shard_map/ppermute | solution.py:227
  44.9 3.8 %collective-permute-done.3.got2 = bf16[19,16,128]{2,1,0:T(8,128)(2,1)S(1)} collective-permute-done((bf16[19,16,128]{2,1,0:T(8,128)(2,1)S(1)}, bf16[19,16,128]{2,1,0:T(8,128)(2,1)S(1)}, u32[]{:S(2)}, u32[]{:S(2)}) %collective-permute-start.3) | collective-permute-done | bytes 77856 | tf_op jit(solution)/shard_map/ppermute | solution.py:227
  48.8 2.0 %collective-permute-done.2.got1 = bf16[19,16,128]{2,1,0:T(8,128)(2,1)S(1)} collective-permute-done((bf16[19,16,128]{2,1,0:T(8,128)(2,1)S(1)}, bf16[19,16,128]{2,1,0:T(8,128)(2,1)S(1)}, u32[]{:S(2)}, u32[]{:S(2)}) %collective-permute-start.2) | collective-permute-done | bytes 77856 | tf_op jit(solution)/shard_map/ppermute | solution.py:227
  51.0 0.6 %pad_add_fusion.top_at = s32[16]{0:T(128)} fusion(s32[4]{0:T(128)S(1)} %convert_reduce_fusion, s32[4]{0:T(128)S(1)} %convert_reduce_fusion.1, s32[4]{0:T(128)S(1)} %convert_reduce_fusion.2, s32[4]{0:T(128)S(1)} %copy-done.6), kind=kLoop, calls=%fused_computation.7 | loop fusion | flops 48 | bytes 128 | tf_op jit(solution)/shard_map/concatenate | solution.py:229
  51.5 1.1 %all-to-all-done.roots = bf16[64,8,128]{2,1,0:T(8,128)(2,1)S(1)} async-done(((bf16[64,8,128]{2,1,0:T(8,128)(2,1)}), bf16[64,8,128]{2,1,0:T(8,128)(2,1)S(1)}, u32[]{:S(2)}, u32[]{:S(2)}) %all-to-all-start) | async-done | bytes 131104 | tf_op jit(solution)/shard_map/all_to_all | solution.py:178
  52.7 0.6 %copy-done = bf16[64,8,128]{2,1,0:T(8,128)(2,1)} copy-done((bf16[64,8,128]{2,1,0:T(8,128)(2,1)}, bf16[64,8,128]{2,1,0:T(8,128)(2,1)S(1)}, u32[]{:S(2)}) %copy-start) | copy-done | bytes 131096
  53.3 2.5 %final.1 = bf16[16,16,128]{2,1,0:T(8,128)(2,1)} custom-call(s32[16]{0:T(128)} %pad_add_fusion.top_at, bf16[64,8,128]{2,1,0:T(8,128)(2,1)} %copy-done, bf16[33,32,128]{2,1,0:T(8,128)(2,1)} %reshape.35.far, bf16[64,4096]{1,0:T(8,128)(2,1)} %top_operator.1.operator, f32[16,16,128]{2,1,0:T(8,128)} %get-tuple-element.16.kept, bf16[19,16,128]{2,1,0:T(8,128)(2,1)} %copy-done.5, ...), custom_call_target="tpu_custom_call" | custom-call | tf_op jit(solution)/shard_map/final/pallas_call | solution.py:232
  (30 shorter events, 1.7 us)
Async XLA Ops:
  2.4 13.7 %collective-permute-start = (bf16[40,32,128]{2,1,0:T(8,128)(2,1)}, bf16[40,32,128]{2,1,0:T(8,128)(2,1)S(1)}, u32[]{:S(2)}, u32[]{:S(2)}) collective-permute-start(bf16[40,32,128]{2,1,0:T(8,128)(2,1)} %get-tuple-element.11.own), channel_id=1, source_target_pairs={{0,4},{4,8},{8,12},{12,16},{16,20},{20,24},{24,28},{28,32},{32,36}... | collective-permute-start | bytes 983048 | tf_op jit(solution)/shard_map/ppermute | solution.py:176
  7.0 9.1 %collective-permute-start.1 = (bf16[40,32,128]{2,1,0:T(8,128)(2,1)}, bf16[40,32,128]{2,1,0:T(8,128)(2,1)S(1)}, u32[]{:S(2)}, u32[]{:S(2)}) collective-permute-start(bf16[40,32,128]{2,1,0:T(8,128)(2,1)} %get-tuple-element.11.own), channel_id=1, source_target_pairs={{4,0},{8,4},{12,8},{16,12},{20,16},{24,20},{28,24},{32,28},{36,32}... | collective-permute-start | bytes 983048 | tf_op jit(solution)/shard_map/ppermute | solution.py:177
  14.2 1.3 %copy-start.8 = (s32[1,4]{1,0:T(1,128)S(1)}, s32[1,4]{1,0:T(1,128)}, u32[]{:S(2)}) copy-start(s32[1,4]{1,0:T(1,128)} %param.21) | copy-start | bytes 52
  16.1 11.6 %copy-start.7 = (bf16[8,128]{1,0:T(8,128)(2,1)S(1)}, bf16[8,128]{1,0:T(8,128)(2,1)}, u32[]{:S(2)}) copy-start(bf16[8,128]{1,0:T(8,128)(2,1)} %get-tuple-element.15) | copy-start | bytes 6148
  16.1 0.7 %copy-start.1 = (bf16[40,32,128]{2,1,0:T(8,128)(2,1)}, bf16[40,32,128]{2,1,0:T(8,128)(2,1)S(1)}, u32[]{:S(2)}) copy-start(bf16[40,32,128]{2,1,0:T(8,128)(2,1)S(1)} %collective-permute-done.before) | copy-start | bytes 983044
  16.8 0.7 %copy-start.2 = (bf16[40,32,128]{2,1,0:T(8,128)(2,1)}, bf16[40,32,128]{2,1,0:T(8,128)(2,1)S(1)}, u32[]{:S(2)}) copy-start(bf16[40,32,128]{2,1,0:T(8,128)(2,1)S(1)} %collective-permute-done.1.after) | copy-start | bytes 983044
  25.1 18.5 %copy-start.10 = (bf16[19,16,128]{2,1,0:T(8,128)(2,1)S(1)}, bf16[19,16,128]{2,1,0:T(8,128)(2,1)}, u32[]{:S(2)}) copy-start(bf16[19,16,128]{2,1,0:T(8,128)(2,1)} %get-tuple-element.13) | copy-start | bytes 233476
  25.1 19.0 %copy-start.9 = (bf16[19,16,128]{2,1,0:T(8,128)(2,1)S(1)}, bf16[19,16,128]{2,1,0:T(8,128)(2,1)}, u32[]{:S(2)}) copy-start(bf16[19,16,128]{2,1,0:T(8,128)(2,1)} %get-tuple-element.12) | copy-start | bytes 233476
  25.1 25.8 %copy-start.6 = (s32[4]{0:T(128)S(1)}, s32[4]{0:T(128)}, u32[]{:S(2)}) copy-start(s32[4]{0:T(128)} %compare_select_fusion.top_at) | copy-start | bytes 52
  25.1 19.6 %collective-permute-start.4 = (bf16[19,16,128]{2,1,0:T(8,128)(2,1)}, bf16[19,16,128]{2,1,0:T(8,128)(2,1)S(1)}, u32[]{:S(2)}, u32[]{:S(2)}) collective-permute-start(bf16[19,16,128]{2,1,0:T(8,128)(2,1)} %get-tuple-element.14), channel_id=1, source_target_pairs={{0,3},{1,0},{2,1},{3,2},{4,7},{5,4},{6,5},{7,6},{8,11},{9,8},{10,9... | collective-permute-start | bytes 233480 | tf_op jit(solution)/shard_map/ppermute | solution.py:227
  28.4 24.3 %all-to-all-start = ((bf16[64,8,128]{2,1,0:T(8,128)(2,1)}), bf16[64,8,128]{2,1,0:T(8,128)(2,1)S(1)}, u32[]{:S(2)}, u32[]{:S(2)}) async-start(bf16[64,8,128]{2,1,0:T(8,128)(2,1)} %broadcast_in_dim.21), calls=%async_computation | async-start | bytes 262144 | tf_op jit(solution)/shard_map/all_to_all | solution.py:178
  43.6 5.0 %collective-permute-start.3 = (bf16[19,16,128]{2,1,0:T(8,128)(2,1)S(1)}, bf16[19,16,128]{2,1,0:T(8,128)(2,1)S(1)}, u32[]{:S(2)}, u32[]{:S(2)}) collective-permute-start(bf16[19,16,128]{2,1,0:T(8,128)(2,1)S(1)} %copy-done.10), channel_id=1, source_target_pairs={{0,2},{1,3},{2,0},{3,1},{4,6},{5,7},{6,4},{7,5},{8,10},{9,11},{10,... | collective-permute-start | bytes 233480 | tf_op jit(solution)/shard_map/ppermute | solution.py:227
  44.1 6.7 %collective-permute-start.2 = (bf16[19,16,128]{2,1,0:T(8,128)(2,1)S(1)}, bf16[19,16,128]{2,1,0:T(8,128)(2,1)S(1)}, u32[]{:S(2)}, u32[]{:S(2)}) collective-permute-start(bf16[19,16,128]{2,1,0:T(8,128)(2,1)S(1)} %copy-done.9), channel_id=1, source_target_pairs={{0,1},{1,2},{2,3},{3,0},{4,5},{5,6},{6,7},{7,4},{8,9},{9,10},{10,1... | collective-permute-start | bytes 233480 | tf_op jit(solution)/shard_map/ppermute | solution.py:227
  44.7 7.9 %copy-start.3 = (bf16[19,16,128]{2,1,0:T(8,128)(2,1)}, bf16[19,16,128]{2,1,0:T(8,128)(2,1)S(1)}, u32[]{:S(2)}) copy-start(bf16[19,16,128]{2,1,0:T(8,128)(2,1)S(1)} %collective-permute-done.4.got3) | copy-start | bytes 233476
  48.7 4.0 %copy-start.4 = (bf16[19,16,128]{2,1,0:T(8,128)(2,1)}, bf16[19,16,128]{2,1,0:T(8,128)(2,1)S(1)}, u32[]{:S(2)}) copy-start(bf16[19,16,128]{2,1,0:T(8,128)(2,1)S(1)} %collective-permute-done.3.got2) | copy-start | bytes 233476
  50.8 1.8 %copy-start.5 = (bf16[19,16,128]{2,1,0:T(8,128)(2,1)}, bf16[19,16,128]{2,1,0:T(8,128)(2,1)S(1)}, u32[]{:S(2)}) copy-start(bf16[19,16,128]{2,1,0:T(8,128)(2,1)S(1)} %collective-permute-done.2.got1) | copy-start | bytes 233476
  52.7 0.7 %copy-start = (bf16[64,8,128]{2,1,0:T(8,128)(2,1)}, bf16[64,8,128]{2,1,0:T(8,128)(2,1)S(1)}, u32[]{:S(2)}) copy-start(bf16[64,8,128]{2,1,0:T(8,128)(2,1)S(1)} %all-to-all-done.roots) | copy-start | bytes 393220

commit v2 on v0

v2 whole, which is shorter than its diff:
```python
import jax
import jax.numpy as jnp
from jax import lax
from jax.experimental import pallas as pl
from jax.experimental.pallas import tpu as pltpu
from jax.sharding import PartitionSpec as P

BF = jnp.bfloat16
F32 = jnp.float32
LEAVES = 32
ROOTS = 64
GROUP = 4
PACKED = LEAVES + LEAVES // GROUP
ROWS = 8
STEPS = 2
PER_STEP = LEAVES // STEPS
AHEAD = 2
NONE = 3 * LEAVES


def dot_nt(a, b):
    return lax.dot_general(a, b, (((1,), (1,)), ((), ())), preferred_element_type=F32)


def dot_nn(a, b):
    return lax.dot_general(a, b, (((1,), (0,)), ((), ())), preferred_element_type=F32)


def two_terms(value):
    high = value.astype(BF)
    return high, (value - high.astype(F32)).astype(BF)


def coef_kernel(level, vectors, basis_in, transfer_in, packed, basis, transfer, spread, wide, sems):
    copies = [
        pltpu.make_async_copy(vectors, packed.at[0:LEAVES], sems.at[0]),
        pltpu.make_async_copy(basis_in, basis, sems.at[1]),
        pltpu.make_async_copy(transfer_in, transfer, sems.at[2]),
    ]
    for copy in copies:
        copy.start()
    for copy in copies:
        copy.wait()
    total = jnp.zeros((32, 32), F32)
    for g in range(LEAVES // GROUP):
        pieces = []
        for m in range(GROUP):
            i = g * GROUP + m
            c = dot_nt(packed[i], basis[i]).astype(BF)
            total = total + dot_nt(c, transfer[i])
            pieces.append(c)
        packed[LEAVES + g] = jnp.concatenate(pieces, axis=1)
    wide[...] = jnp.concatenate([total] * GROUP, axis=1)
    root = wide[pl.ds(pl.multiple_of(level[0] * ROWS, ROWS), ROWS), :].astype(BF)
    twice = jnp.concatenate([root, root], axis=0)
    for t in range(ROOTS // 2):
        spread[t] = twice


def couplings(rows4, lane, row):
    x = jnp.concatenate([rows4[:, p * 128 : (p + 1) * 128] for p in range(8)], axis=0)
    out = x
    for d in range(1, 4):
        turned = jnp.where(row < 4 - d, pltpu.roll(x, 32 - d, 0), pltpu.roll(x, 4 - d, 0))
        out = jnp.where((row + d) % 4 == lane, pltpu.roll(turned, 32 * d, 1), out)
    return out


def near_far_kernel(
    level,
    leaf,
    near_source_in,
    near_count_in,
    far_source_in,
    far_count_in,
    top_source_in,
    top_count,
    own,
    before,
    after,
    blocks_in,
    far_in,
    top_in,
    basis,
    kept,
    out1,
    out2,
    out3,
    top_own,
    names_own,
    near_source,
    near_count,
    far_source,
    far_count,
    top_source,
    vtab,
    ctab,
    prod,
    terms,
    blocks,
    far,
    top,
    sems,
):
    def stream(n):
        part = pl.ds(n * PER_STEP, PER_STEP)
        return pltpu.make_async_copy(blocks_in.at[part], blocks.at[part], sems.at[n])

    small = [
        pltpu.make_async_copy(a, b, sems.at[STEPS + n])
        for n, (a, b) in enumerate(
            (
                (near_source_in, near_source),
                (near_count_in, near_count),
                (far_source_in, far_source),
                (far_count_in, far_count),
                (top_source_in, top_source),
                (top_in, top),
                (far_in, far),
            )
        )
    ]
    for copy in small:
        copy.start()
    for n in range(AHEAD):
        stream(n).start()
    lane = lax.broadcasted_iota(jnp.int32, (32, 128), 1) // 32
    row = lax.broadcasted_iota(jnp.int32, (32, 128), 0) % 4
    for n, part in enumerate((before, own, after)):
        vtab[n * LEAVES : (n + 1) * LEAVES] = part[0:LEAVES]
        for g in range(LEAVES // GROUP):
            tile = part[LEAVES + g].astype(F32)
            turned = [tile] + [pltpu.roll(tile, 32 * k, 1) for k in range(1, GROUP)]
            for m in range(GROUP):
                v = turned[(0 - m) % GROUP]
                for k in range(1, GROUP):
                    v = jnp.where(lane == k, turned[(k - m) % GROUP], v)
                ctab[n * LEAVES + g * GROUP + m] = v.astype(BF)
    vtab[NONE] = jnp.zeros((32, 128), BF)
    ctab[NONE] = jnp.zeros((32, 128), BF)

    me = level[0]
    first = me * 4
    shift = LEAVES - leaf[0] * LEAVES
    for copy in small:
        copy.wait()
    top_f = couplings(top[0].astype(F32), lane, row).astype(BF)
    top_own[...] = top_f
    row8 = lax.broadcasted_iota(jnp.int32, (16, 128), 0)
    names = jnp.full((16, 128), -1, jnp.int32)
    for s in range(4):
        names = jnp.where(row8 == s, jnp.where(first + s < top_count[0], top_source[0, s], -1), names)
    names_own[...] = names[0:8]
    names = names.astype(F32).astype(BF)
    for out in (out1, out2, out3):
        out[LEAVES // 2] = top_f[0:16]
        out[LEAVES // 2 + 1] = top_f[16:32]
        out[LEAVES // 2 + 2] = names

    same = lax.broadcasted_iota(jnp.int32, (128, 128), 0) // 32 == lax.broadcasted_iota(jnp.int32, (128, 128), 1) // 32
    for g in range(LEAVES // GROUP):
        chosen = []
        matrices = []
        for m in range(GROUP):
            i = g * GROUP + m
            far_at = [jnp.where(first + s < far_count[i], far_source[s, i] + shift, NONE) for s in range(4)]
            c = ctab[far_at[0]]
            for s in range(1, 4):
                c = jnp.where(lane == s, ctab[far_at[s]], c)
            chosen.append(c)
            matrices.append(couplings(far[i].astype(F32), lane, row).astype(BF))
        down = dot_nt(jnp.concatenate(chosen, axis=0), jnp.concatenate(matrices, axis=0))
        terms[g] = jnp.concatenate(two_terms(jnp.where(same, down, 0.0)), axis=1)

    @pl.loop(0, STEPS)
    def _(step):
        stream(step).wait()

        @pl.when(step + AHEAD < STEPS)
        def _():
            stream(step + AHEAD).start()

        for h in range(PER_STEP // GROUP):
            g = step * (PER_STEP // GROUP) + h
            b = basis[pl.ds(g * GROUP, GROUP)].reshape(GROUP * 32, 128)
            value = dot_nn(terms[g], jnp.concatenate([b, b], axis=0))
            for m in range(GROUP):
                i = g * GROUP + m
                near_at = [jnp.where(first + s < near_count[i], near_source[s, i] + shift, NONE) for s in range(4)]
                total = value[m * 32 : m * 32 + 32]
                for s in range(0, 4, 2):
                    lhs = jnp.concatenate([vtab[near_at[s]], vtab[near_at[s + 1]]], axis=1)
                    rhs = jnp.concatenate([blocks[i, s], blocks[i, s + 1]], axis=1)
                    total = total + dot_nt(lhs, rhs)
                prod[h * GROUP + m] = total
            for m in range(0, GROUP, 2):
                pair = (step * PER_STEP + h * GROUP + m) // 2

                def rows(k):
                    at = pl.multiple_of(lax.rem(me + k, 4) * ROWS, ROWS)
                    n = h * GROUP + m
                    return jnp.concatenate([prod[n, pl.ds(at, ROWS), :], prod[n + 1, pl.ds(at, ROWS), :]], axis=0)

                kept[pair] = rows(0)
                for k, out in ((1, out1), (2, out2), (3, out3)):
                    out[pair] = rows(k).astype(BF)


def top_operator_kernel(transfer, basis, operator):
    for i in range(LEAVES):
        high, low = two_terms(dot_nn(transfer[i], basis[i]))
        operator[0:32, i * 128 : (i + 1) * 128] = high
        operator[32:64, i * 128 : (i + 1) * 128] = low


def final_kernel(roots, operator, kept, top_own, names_own, got1, got2, got3, out, names_v, names_s, sem):
    others = (got1, got2, got3)
    names_v[0:ROWS] = names_own[...]
    for k, got in enumerate(others):
        names_v[(k + 1) * ROWS : (k + 2) * ROWS] = got[LEAVES // 2 + 2].astype(F32)[0:ROWS].astype(jnp.int32)
    copy = pltpu.make_async_copy(names_v, names_s, sem)
    copy.start()
    for h in range(LEAVES // 2):
        kept[h] = kept[h] + got1[h].astype(F32) + got2[h].astype(F32) + got3[h].astype(F32)
    lane = lax.broadcasted_iota(jnp.int32, (ROWS, 128), 1) // 32
    total = jnp.zeros((ROWS, 32), F32)
    copy.wait()
    for k in range(4):
        c = jnp.zeros((ROWS, 128), F32)
        for s in range(4):
            at = names_s[k * ROWS + s, 0]
            c = jnp.where((lane == s) & (at >= 0), roots[jnp.maximum(at, 0)].astype(F32), c)
        c = c.astype(BF)
        if k == 0:
            total = total + dot_nt(c, top_own[...])
        else:
            got = others[k - 1]
            total = total + dot_nt(c, jnp.concatenate([got[LEAVES // 2], got[LEAVES // 2 + 1]], axis=0))
    high, low = two_terms(total)
    lhs = jnp.concatenate([high, low, high], axis=1)
    for h in range(LEAVES // 2):
        w = operator[:, h * 256 : (h + 1) * 256]
        t = dot_nn(lhs, jnp.concatenate([w[0:32], w[0:32], w[32:64]], axis=0))
        out[h] = (kept[h] + jnp.concatenate([t[:, 0:128], t[:, 128:256]], axis=0)).astype(BF)


SMEM = pl.BlockSpec(memory_space=pltpu.SMEM)
VMEM = pl.BlockSpec(memory_space=pltpu.VMEM)
HBM = pl.BlockSpec(memory_space=pltpu.HBM)
LIMIT = 16 * 1024 * 1024


def held(value):
    return pltpu.with_memory_space_constraint(value, pltpu.VMEM)


def stays(value):
    return pltpu.with_memory_space_constraint(value, pltpu.HBM)


def params(flops):
    return dict(
        compiler_params=pltpu.CompilerParams(vmem_limit_bytes=LIMIT),
        cost_estimate=pl.CostEstimate(flops=flops, bytes_accessed=1 << 20, transcendentals=0),
    )


def gathered(spread):
    return lax.all_to_all(spread, "leaf", 0, 0, tiled=True)


def per_device(
    vectors,
    leaf_basis,
    transfer,
    nearfield_source_leaf,
    near_count,
    nearfield_block_matrix,
    far_source,
    far_count,
    far_block,
    top_source,
    top_count,
    top_block,
):
    level = lax.axis_index("level").astype(jnp.int32).reshape(1)
    leaf = lax.axis_index("leaf").astype(jnp.int32).reshape(1)
    packed, basis, carried, spread = pl.pallas_call(
        coef_kernel,
        out_shape=(
            pltpu.VMEM((PACKED, 32, 128), BF),
            pltpu.VMEM((LEAVES, 32, 128), BF),
            pltpu.VMEM((LEAVES, 32, 32), BF),
            pltpu.VMEM((ROOTS // 2, 2 * ROWS, 128), BF),
        ),
        in_specs=[SMEM] + [HBM] * 3,
        out_specs=(VMEM,) * 4,
        scratch_shapes=[pltpu.VMEM((32, 128), F32), pltpu.SemaphoreType.DMA((3,))],
        name="coefficients",
        **params(1 << 24),
    )(level, stays(vectors), stays(leaf_basis), stays(transfer))

    before = lax.ppermute(packed, "leaf", [(n, n + 1) for n in range(63)])
    after = lax.ppermute(packed, "leaf", [(n + 1, n) for n in range(63)])
    roots = gathered(spread.reshape(ROOTS, ROWS, 128))

    operator = pl.pallas_call(
        top_operator_kernel,
        out_shape=pltpu.VMEM((64, LEAVES * 128), BF),
        in_specs=[VMEM, VMEM],
        out_specs=VMEM,
        name="top_operator",
        **params(1 << 24),
    )(held(carried), held(basis))

    parts = LEAVES // 2
    sent = pltpu.VMEM((parts + 3, 16, 128), BF)
    kept, out1, out2, out3, top_own, names_own = pl.pallas_call(
        near_far_kernel,
        out_shape=(
            pltpu.VMEM((parts, 16, 128), F32),
            sent,
            sent,
            sent,
            pltpu.VMEM((32, 128), BF),
            pltpu.VMEM((ROWS, 128), jnp.int32),
        ),
        in_specs=[SMEM] * 2 + [HBM] * 5 + [SMEM] + [VMEM] * 3 + [HBM] * 3 + [VMEM],
        out_specs=(VMEM,) * 6,
        scratch_shapes=[
            pltpu.SMEM((4, LEAVES), jnp.int32),
            pltpu.SMEM((LEAVES,), jnp.int32),
            pltpu.SMEM((4, LEAVES), jnp.int32),
            pltpu.SMEM((LEAVES,), jnp.int32),
            pltpu.SMEM((1, 4), jnp.int32),
            pltpu.VMEM((NONE + 1, 32, 128), BF),
            pltpu.VMEM((NONE + 1, 32, 128), BF),
            pltpu.VMEM((PER_STEP, 32, 128), F32),
            pltpu.VMEM((LEAVES // GROUP, 128, 256), BF),
            pltpu.VMEM((LEAVES, 4, 128, 128), BF),
            pltpu.VMEM((LEAVES, 4, 1024), BF),
            pltpu.VMEM((1, 4, 1024), BF),
            pltpu.SemaphoreType.DMA((STEPS + 7,)),
        ],
        name="near_far",
        **params(1 << 30),
    )(
        level,
        leaf,
        stays(nearfield_source_leaf.T),
        stays(near_count),
        stays(far_source.T),
        stays(far_count),
        stays(top_source),
        top_count,
        held(packed),
        held(before),
        held(after),
        stays(nearfield_block_matrix),
        stays(far_block),
        stays(top_block),
        held(basis),
    )

    got = {}
    for k, out in ((2, out2), (1, out1), (3, out3)):
        got[k] = lax.ppermute(out, "level", [(n, (n + k) % 4) for n in range(4)])

    result = pl.pallas_call(
        final_kernel,
        out_shape=jax.ShapeDtypeStruct((parts, 16, 128), BF),
        in_specs=[VMEM] * 8,
        out_specs=VMEM,
        scratch_shapes=[
            pltpu.VMEM((4 * ROWS, 128), jnp.int32),
            pltpu.SMEM((4 * ROWS, 128), jnp.int32),
            pltpu.SemaphoreType.DMA,
        ],
        name="final",
        **params(1 << 24),
    )(
        held(roots),
        held(operator),
        held(kept),
        held(top_own),
        held(names_own),
        held(got[1]),
        held(got[2]),
        held(got[3]),
    )
    return result.reshape(LEAVES, ROWS, 128)


def solution(mesh):
    placed = (
        P("leaf", None, None),
        P("leaf", None, None),
        P("leaf", None, None),
        P("leaf", "level"),
        P("leaf"),
        P("leaf", "level", None, None),
        P("leaf", "level"),
        P("leaf"),
        P("leaf", "level", None),
        P("leaf", "level"),
        P("leaf"),
        P("leaf", "level", None),
    )
    return jax.shard_map(
        per_device, mesh=mesh, in_specs=placed, out_specs=P("leaf", "level", None), check_vma=False
    )
```

time: 142 us -> 36.6 us (0.26)
  blocking collectives: 53.8 us -> 0 us
  waiting for transfers between devices: 40.7 us -> 2.32 us
  starting transfers between devices: 7.11 us -> 25 us
  matrix products: 13.6 us -> 0 us
  between operations: 14.2 us -> 0.72 us
  local copies, waits for them, and re-layouts: 9.56 us -> 0 us
  Pallas kernels: 0 us -> 8.16 us
  other arithmetic: 2.26 us -> 0 us
    all_gather x1 -> x0, blocking collectives: 53.8 us -> none  [per_device(): lax.all_gather(root_coef[None], 'leaf', axis=0, tiled=True)]
    reduce_scatter x2 -> x0, waiting for transfers between devices: 40.6 us -> none  [the longest x1 26.3 us: per_device(): lax.psum_scatter(near_sum, 'level', scatter_dimension=1, tiled=True)]
    dot_general x7 -> x0, matrix products: 13.6 us -> none  [the longest x1 4.51 us: per_device(): jnp.einsum('nsrq,nspq->nrp', near_gathered, nearfield_block_matrix, prefe...]
    all_to_all x0 -> x1, starting transfers between devices: none -> 13 us  [gathered(): return lax.all_to_all(spread, 'leaf', 0, 0, tiled=True)]
    pallas_call x0 -> x4, Pallas kernels: none -> 8.16 us  [the longest x1 3.64 us: per_device(): pl.pallas_call(near_far_kernel, out_shape=(pltpu.VMEM((parts, 16, 128), F...]
    ppermute x2 -> x5, starting transfers between devices: 7.07 us -> 12 us  [the longest x1 5.15 us: per_device(): after = lax.ppermute(packed, 'leaf', [(n + 1, n) for n in range(63)])]
    reshape x3 -> x0, local copies, waits for them, and re-layouts: 3.21 us -> none  [the longest x1 1.82 us: per_device(): far_blocks = far_block.reshape(leaves, far_slots, ranks, ranks)]
    gather x3 -> x0, local copies, waits for them, and re-layouts: 2.98 us -> none  [the longest x1 1.66 us: per_device(): coef_rows[far_local] * far_active[:, :, None, None].astype(jnp.bfloat16)]
  transfers between devices with their start and end apart: 4 -> 6, of which waited for: 2 -> 3; matrix products, arithmetic and copies ran while one was open for 10% -> 0% of each run, Pallas kernels for 0% -> 11%
where the time goes in v2:
time: 36.6 us; the launch traced here: 36.2 us
  starting transfers between devices  25 us (68%)
  Pallas kernels  8.16 us (22%)
  waiting for transfers between devices  2.32 us (6%)
  between operations  0.72 us (2%)
    all_to_all x1, starting transfers between devices, gathered(): return lax.all_to_all(spread, 'leaf', 0, 0, tiled=True)  13 us
    ppermute x1, starting transfers between devices, per_device(): after = lax.ppermute(packed, 'leaf', [(n + 1, n) for n in range(63)])  5.15 us
    ppermute x3, starting transfers between devices, per_device(): got[k] = lax.ppermute(out, 'level', [(n, (n + k) % 4) for n in range(4)])  4.89 us
    pallas_call x1, Pallas kernels, per_device(): pl.pallas_call(near_far_kernel, out_shape=(pltpu.VMEM((parts, 16, 128), F...  3.64 us
    pallas_call x1, Pallas kernels, per_device(): pl.pallas_call(coef_kernel, out_shape=(pltpu.VMEM((PACKED, 32, 128), BF),...  2.4 us
    ppermute x1, starting transfers between devices, per_device(): before = lax.ppermute(packed, 'leaf', [(n, n + 1) for n in range(63)])  1.92 us
    pallas_call x1, Pallas kernels, per_device(): pl.pallas_call(final_kernel, out_shape=jax.ShapeDtypeStruct((parts, 16, 1...  1.9 us
    all_to_all x1, waiting for transfers between devices, gathered(): return lax.all_to_all(spread, 'leaf', 0, 0, tiled=True)  1.67 us
  transfers between devices with their start and end apart: 6, of which 3 were waited for; matrix products, arithmetic and copies ran while one was open for 0% of the time, Pallas kernels for 11%

profile of v2, /device:TPU:1, one launch (start us, length us, event | category | flops | bytes accessed | tf_op | source)
XLA Modules:
  0.0 36.2 jit_solution(8319099891814344237)
XLA Ops:
  0.0 2.4 %coefficients.1 = (bf16[40,32,128]{2,1,0:T(8,128)(2,1)S(1)}, bf16[32,32,128]{2,1,0:T(8,128)(2,1)S(1)}, bf16[32,32,32]{2,1,0:T(8,128)(2,1)S(1)}, bf16[32,16,128]{2,1,0:T(8,128)(2,1)}) custom-call(s32[1]{0:T(128)} %bitcast.level, bf16[32,32,128]{2,1,0:T(8,128)(2,1)} %vectors.1, bf16[32,32,128]{2,1,0:T(8,128)(2,1)} %basis_in.1, bf16[32,32,32]{2,1,0:T(8,128)(2,1)} %transfer_in.1), custom_call_target="tpu_custom_call" | custom-call | flops 16777216 | bytes 1048576 | tf_op jit(solution)/shard_map/coefficients/pallas_call | solution.py:288
  2.4 5.1 %collective-permute-start.1 = (bf16[40,32,128]{2,1,0:T(8,128)(2,1)S(1)}, bf16[40,32,128]{2,1,0:T(8,128)(2,1)S(1)}, u32[]{:S(2)}, u32[]{:S(2)}) collective-permute-start(bf16[40,32,128]{2,1,0:T(8,128)(2,1)S(1)} %get-tuple-element.18.own), channel_id=1, source_target_pairs={{4,0},{8,4},{12,8},{16,12},{20,16},{24,20},{28,24},{32,28},{36,32}... | collective-permute-start | bytes 983048 | tf_op jit(solution)/shard_map/ppermute | solution.py:304
  7.6 1.9 %collective-permute-start = (bf16[40,32,128]{2,1,0:T(8,128)(2,1)S(1)}, bf16[40,32,128]{2,1,0:T(8,128)(2,1)S(1)}, u32[]{:S(2)}, u32[]{:S(2)}) collective-permute-start(bf16[40,32,128]{2,1,0:T(8,128)(2,1)S(1)} %get-tuple-element.18.own), channel_id=1, source_target_pairs={{0,4},{4,8},{8,12},{12,16},{16,20},{20,24},{24,28},{28,32},{32,36}... | collective-permute-start | bytes 983048 | tf_op jit(solution)/shard_map/ppermute | solution.py:303
  9.5 13.0 %all-to-all-start = ((bf16[64,8,128]{2,1,0:T(8,128)(2,1)}), bf16[64,8,128]{2,1,0:T(8,128)(2,1)S(1)}, u32[]{:S(2)}, u32[]{:S(2)}) async-start(bf16[64,8,128]{2,1,0:T(8,128)(2,1)} %bitcast.1), calls=%async_computation | async-start | bytes 262144 | tf_op jit(solution)/shard_map/all_to_all | solution.py:269
  23.2 0.0 collective-permute-done.1.after
  23.2 0.0 collective-permute-done.before
  23.2 3.6 %near_far.1 = (f32[16,16,128]{2,1,0:T(8,128)S(1)}, bf16[19,16,128]{2,1,0:T(8,128)(2,1)S(1)}, bf16[19,16,128]{2,1,0:T(8,128)(2,1)S(1)}, bf16[19,16,128]{2,1,0:T(8...) custom-call(s32[1]{0:T(128)} %bitcast.level, s32[1]{0:T(128)} %bitcast.2.leaf, s32[4,32]{1,0:T(4,128)} %bitcast.6, ...), custom_call_target="tpu_custom_call" | custom-call | flops 1073741824 | bytes 1048576 | tf_op jit(solution)/shard_map/near_far/pallas_call | solution.py:318
  26.9 1.3 %collective-permute-start.2 = (bf16[19,16,128]{2,1,0:T(8,128)(2,1)S(1)}, bf16[19,16,128]{2,1,0:T(8,128)(2,1)S(1)}, u32[]{:S(2)}, u32[]{:S(2)}) collective-permute-start(bf16[19,16,128]{2,1,0:T(8,128)(2,1)S(1)} %get-tuple-element.22), channel_id=1, source_target_pairs={{0,1},{1,2},{2,3},{3,0},{4,5},{5,6},{6,7},{7,4},{8,9},{9,10},{10,1... | collective-permute-start | bytes 233480 | tf_op jit(solution)/shard_map/ppermute | solution.py:367
  28.1 2.5 %collective-permute-start.3 = (bf16[19,16,128]{2,1,0:T(8,128)(2,1)S(1)}, bf16[19,16,128]{2,1,0:T(8,128)(2,1)S(1)}, u32[]{:S(2)}, u32[]{:S(2)}) collective-permute-start(bf16[19,16,128]{2,1,0:T(8,128)(2,1)S(1)} %get-tuple-element.23), channel_id=1, source_target_pairs={{0,2},{1,3},{2,0},{3,1},{4,6},{5,7},{6,4},{7,5},{8,10},{9,11},{10,... | collective-permute-start | bytes 233480 | tf_op jit(solution)/shard_map/ppermute | solution.py:367
  30.6 1.1 %collective-permute-start.4 = (bf16[19,16,128]{2,1,0:T(8,128)(2,1)S(1)}, bf16[19,16,128]{2,1,0:T(8,128)(2,1)S(1)}, u32[]{:S(2)}, u32[]{:S(2)}) collective-permute-start(bf16[19,16,128]{2,1,0:T(8,128)(2,1)S(1)} %get-tuple-element.24), channel_id=1, source_target_pairs={{0,3},{1,0},{2,1},{3,2},{4,7},{5,4},{6,5},{7,6},{8,11},{9,8},{10,9... | collective-permute-start | bytes 233480 | tf_op jit(solution)/shard_map/ppermute | solution.py:367
  31.7 0.2 top_operator.1.operator
  32.0 1.7 %all-to-all-done.roots = bf16[64,8,128]{2,1,0:T(8,128)(2,1)S(1)} async-done(((bf16[64,8,128]{2,1,0:T(8,128)(2,1)}), bf16[64,8,128]{2,1,0:T(8,128)(2,1)S(1)}, u32[]{:S(2)}, u32[]{:S(2)}) %all-to-all-start) | async-done | bytes 131104 | tf_op jit(solution)/shard_map/all_to_all | solution.py:269
  33.6 0.0 collective-permute-done.2.got1
  33.6 0.3 collective-permute-done.3.got2
  34.0 0.3 collective-permute-done.4.got3
  34.3 1.9 %final.1 = bf16[16,16,128]{2,1,0:T(8,128)(2,1)} custom-call(bf16[64,8,128]{2,1,0:T(8,128)(2,1)S(1)} %all-to-all-done.roots, bf16[64,4096]{1,0:T(8,128)(2,1)S(1)} %top_operator.1.operator, f32[16,16,128]{2,1,0:T(8,128)S(1)} %get-tuple-element.19.kept, bf16[32,128]{1,0:T(8,128)(2,1)S(1)} %get-tuple-element.20.top_own, ...), custom_call_target="tpu_custom_call" | custom-call | flops 16777216 | bytes 1048576 | tf_op jit(solution)/shard_map/final/pallas_call | solution.py:369
Async XLA Ops:
  2.4 20.8 %collective-permute-start.1 = (bf16[40,32,128]{2,1,0:T(8,128)(2,1)S(1)}, bf16[40,32,128]{2,1,0:T(8,128)(2,1)S(1)}, u32[]{:S(2)}, u32[]{:S(2)}) collective-permute-start(bf16[40,32,128]{2,1,0:T(8,128)(2,1)S(1)} %get-tuple-element.18.own), channel_id=1, source_target_pairs={{4,0},{8,4},{12,8},{16,12},{20,16},{24,20},{28,24},{32,28},{36,32}... | collective-permute-start | bytes 983048 | tf_op jit(solution)/shard_map/ppermute | solution.py:304
  7.6 15.6 %collective-permute-start = (bf16[40,32,128]{2,1,0:T(8,128)(2,1)S(1)}, bf16[40,32,128]{2,1,0:T(8,128)(2,1)S(1)}, u32[]{:S(2)}, u32[]{:S(2)}) collective-permute-start(bf16[40,32,128]{2,1,0:T(8,128)(2,1)S(1)} %get-tuple-element.18.own), channel_id=1, source_target_pairs={{0,4},{4,8},{8,12},{12,16},{16,20},{20,24},{24,28},{28,32},{32,36}... | collective-permute-start | bytes 983048 | tf_op jit(solution)/shard_map/ppermute | solution.py:303
  9.5 24.2 %all-to-all-start = ((bf16[64,8,128]{2,1,0:T(8,128)(2,1)}), bf16[64,8,128]{2,1,0:T(8,128)(2,1)S(1)}, u32[]{:S(2)}, u32[]{:S(2)}) async-start(bf16[64,8,128]{2,1,0:T(8,128)(2,1)} %bitcast.1), calls=%async_computation | async-start | bytes 262144 | tf_op jit(solution)/shard_map/all_to_all | solution.py:269
  26.9 6.8 %collective-permute-start.2 = (bf16[19,16,128]{2,1,0:T(8,128)(2,1)S(1)}, bf16[19,16,128]{2,1,0:T(8,128)(2,1)S(1)}, u32[]{:S(2)}, u32[]{:S(2)}) collective-permute-start(bf16[19,16,128]{2,1,0:T(8,128)(2,1)S(1)} %get-tuple-element.22), channel_id=1, source_target_pairs={{0,1},{1,2},{2,3},{3,0},{4,5},{5,6},{6,7},{7,4},{8,9},{9,10},{10,1... | collective-permute-start | bytes 233480 | tf_op jit(solution)/shard_map/ppermute | solution.py:367
  28.1 5.8 %collective-permute-start.3 = (bf16[19,16,128]{2,1,0:T(8,128)(2,1)S(1)}, bf16[19,16,128]{2,1,0:T(8,128)(2,1)S(1)}, u32[]{:S(2)}, u32[]{:S(2)}) collective-permute-start(bf16[19,16,128]{2,1,0:T(8,128)(2,1)S(1)} %get-tuple-element.23), channel_id=1, source_target_pairs={{0,2},{1,3},{2,0},{3,1},{4,6},{5,7},{6,4},{7,5},{8,10},{9,11},{10,... | collective-permute-start | bytes 233480 | tf_op jit(solution)/shard_map/ppermute | solution.py:367
  30.6 3.7 %collective-permute-start.4 = (bf16[19,16,128]{2,1,0:T(8,128)(2,1)S(1)}, bf16[19,16,128]{2,1,0:T(8,128)(2,1)S(1)}, u32[]{:S(2)}, u32[]{:S(2)}) collective-permute-start(bf16[19,16,128]{2,1,0:T(8,128)(2,1)S(1)} %get-tuple-element.24), channel_id=1, source_target_pairs={{0,3},{1,0},{2,1},{3,2},{4,7},{5,4},{6,5},{7,6},{8,11},{9,8},{10,9... | collective-permute-start | bytes 233480 | tf_op jit(solution)/shard_map/ppermute | solution.py:367

commit v3 on v2

--- a/solution.py
+++ b/solution.py
@@ -53,7 +53,7 @@
     wide[...] = jnp.concatenate([total] * GROUP, axis=1)
     root = wide[pl.ds(pl.multiple_of(level[0] * ROWS, ROWS), ROWS), :].astype(BF)
     twice = jnp.concatenate([root, root], axis=0)
-    for t in range(ROOTS // 2):
+    for t in range(ROOTS // 4):
         spread[t] = twice
 
 
@@ -76,8 +76,8 @@
     top_source_in,
     top_count,
     own,
-    before,
-    after,
+    inside,
+    outside,
     blocks_in,
     far_in,
     top_in,
@@ -126,8 +126,9 @@
         stream(n).start()
     lane = lax.broadcasted_iota(jnp.int32, (32, 128), 1) // 32
     row = lax.broadcasted_iota(jnp.int32, (32, 128), 0) % 4
-    for n, part in enumerate((before, own, after)):
-        vtab[n * LEAVES : (n + 1) * LEAVES] = part[0:LEAVES]
+    odd = leaf[0] % 2
+    for n, part in ((1, own), (2 - 2 * odd, inside), (2 * odd, outside)):
+        vtab[pl.ds(n * LEAVES, LEAVES)] = part[0:LEAVES]
         for g in range(LEAVES // GROUP):
             tile = part[LEAVES + g].astype(F32)
             turned = [tile] + [pltpu.roll(tile, 32 * k, 1) for k in range(1, GROUP)]
@@ -149,7 +150,7 @@
     row8 = lax.broadcasted_iota(jnp.int32, (16, 128), 0)
     names = jnp.full((16, 128), -1, jnp.int32)
     for s in range(4):
-        names = jnp.where(row8 == s, jnp.where(first + s < top_count[0], top_source[0, s], -1), names)
+        names = jnp.where(row8 == s, jnp.where(first + s < top_count[0], place(top_source[0, s], leaf[0]), -1), names)
     names_own[...] = names[0:8]
     names = names.astype(F32).astype(BF)
     for out in (out1, out2, out3):
@@ -197,7 +198,7 @@
                 pair = (step * PER_STEP + h * GROUP + m) // 2
 
                 def rows(k):
-                    at = pl.multiple_of(lax.rem(me + k, 4) * ROWS, ROWS)
+                    at = pl.multiple_of((me ^ k) * ROWS, ROWS)
                     n = h * GROUP + m
                     return jnp.concatenate([prod[n, pl.ds(at, ROWS), :], prod[n + 1, pl.ds(at, ROWS), :]], axis=0)
 
@@ -213,23 +214,23 @@
         operator[32:64, i * 128 : (i + 1) * 128] = low
 
 
-def final_kernel(roots, operator, kept, top_own, names_own, got1, got2, got3, out, names_v, names_s, sem):
+def final_kernel(roots, other_roots, operator, kept, top_own, names_own, got2, got1, got3, out):
     others = (got1, got2, got3)
-    names_v[0:ROWS] = names_own[...]
-    for k, got in enumerate(others):
-        names_v[(k + 1) * ROWS : (k + 2) * ROWS] = got[LEAVES // 2 + 2].astype(F32)[0:ROWS].astype(jnp.int32)
-    copy = pltpu.make_async_copy(names_v, names_s, sem)
-    copy.start()
+    tiles = [names_own[...].astype(F32)]
+    for got in others:
+        tiles.append(got[LEAVES // 2 + 2].astype(F32)[0:ROWS])
     for h in range(LEAVES // 2):
         kept[h] = kept[h] + got1[h].astype(F32) + got2[h].astype(F32) + got3[h].astype(F32)
     lane = lax.broadcasted_iota(jnp.int32, (ROWS, 128), 1) // 32
     total = jnp.zeros((ROWS, 32), F32)
-    copy.wait()
     for k in range(4):
         c = jnp.zeros((ROWS, 128), F32)
         for s in range(4):
-            at = names_s[k * ROWS + s, 0]
-            c = jnp.where((lane == s) & (at >= 0), roots[jnp.maximum(at, 0)].astype(F32), c)
+            at = jnp.max(tiles[k][s : s + 1]).astype(jnp.int32)
+            spot = jnp.maximum(at, 0)
+            index = spot % (ROOTS // 2)
+            tile = jnp.where(spot < ROOTS // 2, roots[index].astype(F32), other_roots[index].astype(F32))
+            c = jnp.where((lane == s) & (at >= 0), tile, c)
         c = c.astype(BF)
         if k == 0:
             total = total + dot_nt(c, top_own[...])
@@ -266,7 +267,12 @@
 
 
 def gathered(spread):
-    return lax.all_to_all(spread, "leaf", 0, 0, tiled=True)
+    halves = [[n for n in range(ROOTS) if n // 4 % 2 == h] for h in range(2)]
+    return lax.all_to_all(spread, "leaf", 0, 0, tiled=True, axis_index_groups=halves)
+
+
+def place(source, leaf):
+    return ((source ^ leaf) // 4 % 2) * (ROOTS // 2) + source // 8 * 4 + source % 4
 
 
 def per_device(
@@ -291,7 +297,7 @@
             pltpu.VMEM((PACKED, 32, 128), BF),
             pltpu.VMEM((LEAVES, 32, 128), BF),
             pltpu.VMEM((LEAVES, 32, 32), BF),
-            pltpu.VMEM((ROOTS // 2, 2 * ROWS, 128), BF),
+            pltpu.VMEM((ROOTS // 4, 2 * ROWS, 128), BF),
         ),
         in_specs=[SMEM] + [HBM] * 3,
         out_specs=(VMEM,) * 4,
@@ -300,9 +306,9 @@
         **params(1 << 24),
     )(level, stays(vectors), stays(leaf_basis), stays(transfer))
 
-    before = lax.ppermute(packed, "leaf", [(n, n + 1) for n in range(63)])
-    after = lax.ppermute(packed, "leaf", [(n + 1, n) for n in range(63)])
-    roots = gathered(spread.reshape(ROOTS, ROWS, 128))
+    inside = lax.ppermute(packed, "leaf", [(n, n ^ 1) for n in range(64)])
+    outside = lax.ppermute(packed, "leaf", [(n, ((n + 1) ^ 1) - 1) for n in range(1, 63)])
+    roots = gathered(spread.reshape(ROOTS // 2, ROWS, 128))
 
     operator = pl.pallas_call(
         top_operator_kernel,
@@ -354,8 +360,8 @@
         stays(top_source),
         top_count,
         held(packed),
-        held(before),
-        held(after),
+        held(inside),
+        held(outside),
         stays(nearfield_block_matrix),
         stays(far_block),
         stays(top_block),
@@ -364,28 +370,26 @@
 
     got = {}
     for k, out in ((2, out2), (1, out1), (3, out3)):
-        got[k] = lax.ppermute(out, "level", [(n, (n + k) % 4) for n in range(4)])
+        got[k] = lax.ppermute(out, "level", [(n, n ^ k) for n in range(4)])
+
+    other_roots = lax.ppermute(roots, "leaf", [(n, n ^ 6) for n in range(ROOTS)])
 
     result = pl.pallas_call(
         final_kernel,
         out_shape=jax.ShapeDtypeStruct((parts, 16, 128), BF),
-        in_specs=[VMEM] * 8,
+        in_specs=[VMEM] * 9,
         out_specs=VMEM,
-        scratch_shapes=[
-            pltpu.VMEM((4 * ROWS, 128), jnp.int32),
-            pltpu.SMEM((4 * ROWS, 128), jnp.int32),
-            pltpu.SemaphoreType.DMA,
-        ],
         name="final",
         **params(1 << 24),
     )(
         held(roots),
+        held(other_roots),
         held(operator),
         held(kept),
         held(top_own),
         held(names_own),
+        held(got[2]),
         held(got[1]),
-        held(got[2]),
         held(got[3]),
     )
     return result.reshape(LEAVES, ROWS, 128)

time: 36.6 us -> 32.1 us (0.88)
  starting transfers between devices: 25 us -> 20.2 us
  waiting for transfers between devices: 2.32 us -> 3.37 us
  Pallas kernels: 8.16 us -> 7.55 us
    all_to_all x1, starting transfers between devices: 13 us -> 10 us  [gathered(): lax.all_to_all(spread, 'leaf', 0, 0, tiled=True, axis_index_groups=halves)]
    ppermute x5 -> x6, waiting for transfers between devices: 0.65 us -> 3.1 us  [the longest x1 3.09 us: per_device(): lax.ppermute(roots, 'leaf', [(n, n ^ 6) for n in range(ROOTS)])]
    ppermute x5 -> x6, starting transfers between devices: 12 us -> 10.2 us  [the longest x3 3.69 us: per_device(): got[k] = lax.ppermute(out, 'level', [(n, n ^ k) for n in range(4)])]
    all_to_all x1, waiting for transfers between devices: 1.67 us -> 0.26 us  [gathered(): lax.all_to_all(spread, 'leaf', 0, 0, tiled=True, axis_index_groups=halves)]
    pallas_call x1, Pallas kernels: 1.9 us -> 1.27 us  [per_device(): pl.pallas_call(final_kernel, out_shape=jax.ShapeDtypeStruct((parts, 16, 1...]
  transfers between devices with their start and end apart: 6 -> 7, of which waited for: 3 -> 2; matrix products, arithmetic and copies ran while one was open for 0% -> 0% of each run, Pallas kernels for 11% -> 12%
where the time goes in v3:
time: 32.1 us; the launch traced here: 31.9 us
  starting transfers between devices  20.2 us (63%)
  Pallas kernels  7.55 us (24%)
  waiting for transfers between devices  3.37 us (10%)
  between operations  0.72 us (2%)
    all_to_all x1, starting transfers between devices, gathered(): lax.all_to_all(spread, 'leaf', 0, 0, tiled=True, axis_index_groups=halves)  10 us
    ppermute x3, starting transfers between devices, per_device(): got[k] = lax.ppermute(out, 'level', [(n, n ^ k) for n in range(4)])  3.69 us
    pallas_call x1, Pallas kernels, per_device(): pl.pallas_call(near_far_kernel, out_shape=(pltpu.VMEM((parts, 16, 128), F...  3.69 us
    ppermute x1, starting transfers between devices, per_device(): inside = lax.ppermute(packed, 'leaf', [(n, n ^ 1) for n in range(64)])  3.33 us
    ppermute x1, waiting for transfers between devices, per_device(): lax.ppermute(roots, 'leaf', [(n, n ^ 6) for n in range(ROOTS)])  3.09 us
    pallas_call x1, Pallas kernels, per_device(): pl.pallas_call(coef_kernel, out_shape=(pltpu.VMEM((PACKED, 32, 128), BF),...  2.37 us
    ppermute x1, starting transfers between devices, per_device(): lax.ppermute(packed, 'leaf', [(n, (n + 1 ^ 1) - 1) for n in range(1, 63)])  1.91 us
    ppermute x1, starting transfers between devices, per_device(): lax.ppermute(roots, 'leaf', [(n, n ^ 6) for n in range(ROOTS)])  1.3 us
  transfers between devices with their start and end apart: 7, of which 2 were waited for; matrix products, arithmetic and copies ran while one was open for 0% of the time, Pallas kernels for 12%

profile of v3, /device:TPU:1, one launch (start us, length us, event | category | flops | bytes accessed | tf_op | source)
XLA Modules:
  0.0 31.9 jit_solution(5778957886010784332)
XLA Ops:
  0.0 2.4 %coefficients.1 = (bf16[40,32,128]{2,1,0:T(8,128)(2,1)S(1)}, bf16[32,32,128]{2,1,0:T(8,128)(2,1)S(1)}, bf16[32,32,32]{2,1,0:T(8,128)(2,1)S(1)}, bf16[16,16,128]{2,1,0:T(8,128)(2,1)}) custom-call(s32[1]{0:T(128)} %bitcast.level, bf16[32,32,128]{2,1,0:T(8,128)(2,1)} %vectors.1, bf16[32,32,128]{2,1,0:T(8,128)(2,1)} %basis_in.1, bf16[32,32,32]{2,1,0:T(8,128)(2,1)} %transfer_in.1), custom_call_target="tpu_custom_call" | custom-call | flops 16777216 | bytes 1048576 | tf_op jit(solution)/shard_map/coefficients/pallas_call | solution.py:294
  2.4 3.3 %collective-permute-start.1 = (bf16[40,32,128]{2,1,0:T(8,128)(2,1)S(1)}, bf16[40,32,128]{2,1,0:T(8,128)(2,1)S(1)}, u32[]{:S(2)}, u32[]{:S(2)}) collective-permute-start(bf16[40,32,128]{2,1,0:T(8,128)(2,1)S(1)} %get-tuple-element.18.own), channel_id=1, source_target_pairs={{0,4},{4,0},{8,12},{12,8},{16,20},{20,16},{24,28},{28,24},{32,36},... | collective-permute-start | bytes 983048 | tf_op jit(solution)/shard_map/ppermute | solution.py:309
  5.7 1.9 %collective-permute-start.2 = (bf16[40,32,128]{2,1,0:T(8,128)(2,1)S(1)}, bf16[40,32,128]{2,1,0:T(8,128)(2,1)S(1)}, u32[]{:S(2)}, u32[]{:S(2)}) collective-permute-start(bf16[40,32,128]{2,1,0:T(8,128)(2,1)S(1)} %get-tuple-element.18.own), channel_id=1, source_target_pairs={{4,8},{8,4},{12,16},{16,12},{20,24},{24,20},{28,32},{32,28},{36,40... | collective-permute-start | bytes 983048 | tf_op jit(solution)/shard_map/ppermute | solution.py:310
  7.6 10.0 %all-to-all-start = ((bf16[32,8,128]{2,1,0:T(8,128)(2,1)}), bf16[32,8,128]{2,1,0:T(8,128)(2,1)S(1)}, u32[]{:S(2)}, u32[]{:S(2)}) async-start(bf16[32,8,128]{2,1,0:T(8,128)(2,1)} %bitcast.1), calls=%async_computation | async-start | bytes 131072 | tf_op jit(solution)/shard_map/all_to_all | solution.py:271
  18.3 0.0 collective-permute-done.1.inside
  18.3 0.0 collective-permute-done.2.outside
  18.3 3.7 %near_far.1 = (f32[16,16,128]{2,1,0:T(8,128)S(1)}, bf16[19,16,128]{2,1,0:T(8,128)(2,1)S(1)}, bf16[19,16,128]{2,1,0:T(8,128)(2,1)S(1)}, bf16[19,16,128]{2,1,0:T(8...) custom-call(s32[1]{0:T(128)} %bitcast.level, s32[1]{0:T(128)} %bitcast.2.leaf, s32[4,32]{1,0:T(4,128)} %bitcast.6, ...), custom_call_target="tpu_custom_call" | custom-call | flops 1073741824 | bytes 1048576 | tf_op jit(solution)/shard_map/near_far/pallas_call | solution.py:324
  22.0 2.8 %collective-permute-start.3 = (bf16[19,16,128]{2,1,0:T(8,128)(2,1)S(1)}, bf16[19,16,128]{2,1,0:T(8,128)(2,1)S(1)}, u32[]{:S(2)}, u32[]{:S(2)}) collective-permute-start(bf16[19,16,128]{2,1,0:T(8,128)(2,1)S(1)} %get-tuple-element.22), channel_id=1, source_target_pairs={{0,2},{1,3},{2,0},{3,1},{4,6},{5,7},{6,4},{7,5},{8,10},{9,11},{10,... | collective-permute-start | bytes 233480 | tf_op jit(solution)/shard_map/ppermute | solution.py:373
  24.8 0.3 collective-permute-start.4
  25.2 0.6 %collective-permute-start.5 = (bf16[19,16,128]{2,1,0:T(8,128)(2,1)S(1)}, bf16[19,16,128]{2,1,0:T(8,128)(2,1)S(1)}, u32[]{:S(2)}, u32[]{:S(2)}) collective-permute-start(bf16[19,16,128]{2,1,0:T(8,128)(2,1)S(1)} %get-tuple-element.24), channel_id=1, source_target_pairs={{0,3},{1,2},{2,1},{3,0},{4,7},{5,6},{6,5},{7,4},{8,11},{9,10},{10,... | collective-permute-start | bytes 233480 | tf_op jit(solution)/shard_map/ppermute | solution.py:373
  25.7 0.3 all-to-all-done.roots
  26.0 1.3 %collective-permute-start = (bf16[32,8,128]{2,1,0:T(8,128)(2,1)S(1)}, bf16[32,8,128]{2,1,0:T(8,128)(2,1)S(1)}, u32[]{:S(2)}, u32[]{:S(2)}) collective-permute-start(bf16[32,8,128]{2,1,0:T(8,128)(2,1)S(1)} %all-to-all-done.roots), channel_id=1, source_target_pairs={{0,24},{4,28},{8,16},{12,20},{16,8},{20,12},{24,0},{28,4},{32,56},... | collective-permute-start | bytes 196616 | tf_op jit(solution)/shard_map/ppermute | solution.py:375
  27.3 0.2 top_operator.1.operator
  27.5 3.1 %collective-permute-done.other_roots = bf16[32,8,128]{2,1,0:T(8,128)(2,1)S(1)} collective-permute-done((bf16[32,8,128]{2,1,0:T(8,128)(2,1)S(1)}, bf16[32,8,128]{2,1,0:T(8,128)(2,1)S(1)}, u32[]{:S(2)}, u32[]{:S(2)}) %collective-permute-start) | collective-permute-done | bytes 65568 | tf_op jit(solution)/shard_map/ppermute | solution.py:375
  30.6 0.0 collective-permute-done.3.got2
  30.6 0.0 collective-permute-done.4.got1
  30.6 0.0 collective-permute-done.5.got3
  30.6 1.3 %final.1 = bf16[16,16,128]{2,1,0:T(8,128)(2,1)} custom-call(bf16[32,8,128]{2,1,0:T(8,128)(2,1)S(1)} %all-to-all-done.roots, bf16[32,8,128]{2,1,0:T(8,128)(2,1)S(1)} %collective-permute-done.other_roots, bf16[64,4096]{1,0:T(8,128)(2,1)S(1)} %top_operator.1.operator, f32[16,16,128]{2,1,0:T(8,128)S(1)} %get-tuple-element.19.kept, ...), custom_call_target="tpu_custom_call" | custom-call | flops 16777216 | bytes 1048576 | tf_op jit(solution)/shard_map/final/pallas_call | solution.py:377
Async XLA Ops:
  2.4 15.9 %collective-permute-start.1 = (bf16[40,32,128]{2,1,0:T(8,128)(2,1)S(1)}, bf16[40,32,128]{2,1,0:T(8,128)(2,1)S(1)}, u32[]{:S(2)}, u32[]{:S(2)}) collective-permute-start(bf16[40,32,128]{2,1,0:T(8,128)(2,1)S(1)} %get-tuple-element.18.own), channel_id=1, source_target_pairs={{0,4},{4,0},{8,12},{12,8},{16,20},{20,16},{24,28},{28,24},{32,36},... | collective-permute-start | bytes 983048 | tf_op jit(solution)/shard_map/ppermute | solution.py:309
  5.7 12.6 %collective-permute-start.2 = (bf16[40,32,128]{2,1,0:T(8,128)(2,1)S(1)}, bf16[40,32,128]{2,1,0:T(8,128)(2,1)S(1)}, u32[]{:S(2)}, u32[]{:S(2)}) collective-permute-start(bf16[40,32,128]{2,1,0:T(8,128)(2,1)S(1)} %get-tuple-element.18.own), channel_id=1, source_target_pairs={{4,8},{8,4},{12,16},{16,12},{20,24},{24,20},{28,32},{32,28},{36,40... | collective-permute-start | bytes 983048 | tf_op jit(solution)/shard_map/ppermute | solution.py:310
  7.6 18.3 %all-to-all-start = ((bf16[32,8,128]{2,1,0:T(8,128)(2,1)}), bf16[32,8,128]{2,1,0:T(8,128)(2,1)S(1)}, u32[]{:S(2)}, u32[]{:S(2)}) async-start(bf16[32,8,128]{2,1,0:T(8,128)(2,1)} %bitcast.1), calls=%async_computation | async-start | bytes 131072 | tf_op jit(solution)/shard_map/all_to_all | solution.py:271
  22.0 8.6 %collective-permute-start.3 = (bf16[19,16,128]{2,1,0:T(8,128)(2,1)S(1)}, bf16[19,16,128]{2,1,0:T(8,128)(2,1)S(1)}, u32[]{:S(2)}, u32[]{:S(2)}) collective-permute-start(bf16[19,16,128]{2,1,0:T(8,128)(2,1)S(1)} %get-tuple-element.22), channel_id=1, source_target_pairs={{0,2},{1,3},{2,0},{3,1},{4,6},{5,7},{6,4},{7,5},{8,10},{9,11},{10,... | collective-permute-start | bytes 233480 | tf_op jit(solution)/shard_map/ppermute | solution.py:373
  24.8 5.8 %collective-permute-start.4 = (bf16[19,16,128]{2,1,0:T(8,128)(2,1)S(1)}, bf16[19,16,128]{2,1,0:T(8,128)(2,1)S(1)}, u32[]{:S(2)}, u32[]{:S(2)}) collective-permute-start(bf16[19,16,128]{2,1,0:T(8,128)(2,1)S(1)} %get-tuple-element.23), channel_id=1, source_target_pairs={{0,1},{1,0},{2,3},{3,2},{4,5},{5,4},{6,7},{7,6},{8,9},{9,8},{10,11... | collective-permute-start | bytes 233480 | tf_op jit(solution)/shard_map/ppermute | solution.py:373
  25.2 5.4 %collective-permute-start.5 = (bf16[19,16,128]{2,1,0:T(8,128)(2,1)S(1)}, bf16[19,16,128]{2,1,0:T(8,128)(2,1)S(1)}, u32[]{:S(2)}, u32[]{:S(2)}) collective-permute-start(bf16[19,16,128]{2,1,0:T(8,128)(2,1)S(1)} %get-tuple-element.24), channel_id=1, source_target_pairs={{0,3},{1,2},{2,1},{3,0},{4,7},{5,6},{6,5},{7,4},{8,11},{9,10},{10,... | collective-permute-start | bytes 233480 | tf_op jit(solution)/shard_map/ppermute | solution.py:373
  26.0 4.6 %collective-permute-start = (bf16[32,8,128]{2,1,0:T(8,128)(2,1)S(1)}, bf16[32,8,128]{2,1,0:T(8,128)(2,1)S(1)}, u32[]{:S(2)}, u32[]{:S(2)}) collective-permute-start(bf16[32,8,128]{2,1,0:T(8,128)(2,1)S(1)} %all-to-all-done.roots), channel_id=1, source_target_pairs={{0,24},{4,28},{8,16},{12,20},{16,8},{20,12},{24,0},{28,4},{32,56},... | collective-permute-start | bytes 196616 | tf_op jit(solution)/shard_map/ppermute | solution.py:375

commit v4 on v3

--- a/solution.py
+++ b/solution.py
@@ -31,15 +31,47 @@
     return high, (value - high.astype(F32)).astype(BF)
 
 
-def coef_kernel(level, vectors, basis_in, transfer_in, packed, basis, transfer, spread, wide, sems):
-    copies = [
-        pltpu.make_async_copy(vectors, packed.at[0:LEAVES], sems.at[0]),
-        pltpu.make_async_copy(basis_in, basis, sems.at[1]),
-        pltpu.make_async_copy(transfer_in, transfer, sems.at[2]),
-    ]
+def coef_kernel(
+    vectors,
+    basis_in,
+    transfer_in,
+    far_in,
+    top_in,
+    near_source_in,
+    near_count_in,
+    far_source_in,
+    far_count_in,
+    top_source_in,
+    packed,
+    basis,
+    transfer,
+    root_out,
+    far,
+    top,
+    near_source,
+    near_count,
+    far_source,
+    far_count,
+    top_source,
+    wide,
+    sems,
+):
+    pairs = (
+        (vectors, packed.at[0:LEAVES]),
+        (basis_in, basis),
+        (transfer_in, transfer),
+        (far_in, far),
+        (near_source_in, near_source),
+        (near_count_in, near_count),
+        (far_source_in, far_source),
+        (far_count_in, far_count),
+        (top_in, top),
+        (top_source_in, top_source),
+    )
+    copies = [pltpu.make_async_copy(a, b, sems.at[n]) for n, (a, b) in enumerate(pairs)]
     for copy in copies:
         copy.start()
-    for copy in copies:
+    for copy in copies[:3]:
         copy.wait()
     total = jnp.zeros((32, 32), F32)
     for g in range(LEAVES // GROUP):
@@ -51,10 +83,15 @@
             pieces.append(c)
         packed[LEAVES + g] = jnp.concatenate(pieces, axis=1)
     wide[...] = jnp.concatenate([total] * GROUP, axis=1)
-    root = wide[pl.ds(pl.multiple_of(level[0] * ROWS, ROWS), ROWS), :].astype(BF)
-    twice = jnp.concatenate([root, root], axis=0)
+    root = wide[pl.ds(pl.multiple_of(lax.axis_index("level") * ROWS, ROWS), ROWS), :].astype(BF)
+    root_out[...] = jnp.concatenate([root, root], axis=0)
+    for copy in copies[3:]:
+        copy.wait()
+
+
+def spread_kernel(root, spread):
     for t in range(ROOTS // 4):
-        spread[t] = twice
+        spread[t] = root[...]
 
 
 def couplings(rows4, lane, row):
@@ -67,20 +104,17 @@
 
 
 def near_far_kernel(
-    level,
-    leaf,
     near_source_in,
     near_count_in,
     far_source_in,
     far_count_in,
     top_source_in,
-    top_count,
     own,
+    outside,
     inside,
-    outside,
     blocks_in,
-    far_in,
-    top_in,
+    far,
+    top,
     basis,
     kept,
     out1,
@@ -98,8 +132,6 @@
     prod,
     terms,
     blocks,
-    far,
-    top,
     sems,
 ):
     def stream(n):
@@ -115,8 +147,6 @@
                 (far_source_in, far_source),
                 (far_count_in, far_count),
                 (top_source_in, top_source),
-                (top_in, top),
-                (far_in, far),
             )
         )
     ]
@@ -126,7 +156,10 @@
         stream(n).start()
     lane = lax.broadcasted_iota(jnp.int32, (32, 128), 1) // 32
     row = lax.broadcasted_iota(jnp.int32, (32, 128), 0) % 4
-    odd = leaf[0] % 2
+    me = lax.axis_index("level")
+    leaf = lax.axis_index("leaf")
+    first = me * 4
+    odd = leaf % 2
     for n, part in ((1, own), (2 - 2 * odd, inside), (2 * odd, outside)):
         vtab[pl.ds(n * LEAVES, LEAVES)] = part[0:LEAVES]
         for g in range(LEAVES // GROUP):
@@ -140,17 +173,15 @@
     vtab[NONE] = jnp.zeros((32, 128), BF)
     ctab[NONE] = jnp.zeros((32, 128), BF)
 
-    me = level[0]
-    first = me * 4
-    shift = LEAVES - leaf[0] * LEAVES
+    shift = LEAVES - leaf * LEAVES
     for copy in small:
         copy.wait()
     top_f = couplings(top[0].astype(F32), lane, row).astype(BF)
     top_own[...] = top_f
     row8 = lax.broadcasted_iota(jnp.int32, (16, 128), 0)
-    names = jnp.full((16, 128), -1, jnp.int32)
+    names = jnp.zeros((16, 128), jnp.int32)
     for s in range(4):
-        names = jnp.where(row8 == s, jnp.where(first + s < top_count[0], place(top_source[0, s], leaf[0]), -1), names)
+        names = jnp.where(row8 == s, place(top_source[0, s], leaf), names)
     names_own[...] = names[0:8]
     names = names.astype(F32).astype(BF)
     for out in (out1, out2, out3):
@@ -214,8 +245,9 @@
         operator[32:64, i * 128 : (i + 1) * 128] = low
 
 
-def final_kernel(roots, other_roots, operator, kept, top_own, names_own, got2, got1, got3, out):
+def final_kernel(top_count, roots, other_roots, operator, kept, top_own, names_own, got2, got1, got3, out):
     others = (got1, got2, got3)
+    me = lax.axis_index("level")
     tiles = [names_own[...].astype(F32)]
     for got in others:
         tiles.append(got[LEAVES // 2 + 2].astype(F32)[0:ROWS])
@@ -226,11 +258,11 @@
     for k in range(4):
         c = jnp.zeros((ROWS, 128), F32)
         for s in range(4):
-            at = jnp.max(tiles[k][s : s + 1]).astype(jnp.int32)
-            spot = jnp.maximum(at, 0)
+            spot = jnp.max(tiles[k][s : s + 1]).astype(jnp.int32)
             index = spot % (ROOTS // 2)
             tile = jnp.where(spot < ROOTS // 2, roots[index].astype(F32), other_roots[index].astype(F32))
-            c = jnp.where((lane == s) & (at >= 0), tile, c)
+            live = (me ^ k) * 4 + s < top_count[0]
+            c = jnp.where((lane == s) & live, tile, c)
         c = c.astype(BF)
         if k == 0:
             total = total + dot_nt(c, top_own[...])
@@ -289,25 +321,49 @@
     top_count,
     top_block,
 ):
-    level = lax.axis_index("level").astype(jnp.int32).reshape(1)
-    leaf = lax.axis_index("leaf").astype(jnp.int32).reshape(1)
-    packed, basis, carried, spread = pl.pallas_call(
+    packed, basis, carried, root, far, top, near_at, near_n, far_at, far_n, top_at = pl.pallas_call(
         coef_kernel,
         out_shape=(
             pltpu.VMEM((PACKED, 32, 128), BF),
             pltpu.VMEM((LEAVES, 32, 128), BF),
             pltpu.VMEM((LEAVES, 32, 32), BF),
-            pltpu.VMEM((ROOTS // 4, 2 * ROWS, 128), BF),
+            pltpu.VMEM((2 * ROWS, 128), BF),
+            pltpu.VMEM((LEAVES, 4, 1024), BF),
+            pltpu.VMEM((1, 4, 1024), BF),
+            pltpu.VMEM((4, LEAVES), jnp.int32),
+            pltpu.VMEM((LEAVES,), jnp.int32),
+            pltpu.VMEM((4, LEAVES), jnp.int32),
+            pltpu.VMEM((LEAVES,), jnp.int32),
+            pltpu.VMEM((1, 4), jnp.int32),
         ),
-        in_specs=[SMEM] + [HBM] * 3,
-        out_specs=(VMEM,) * 4,
-        scratch_shapes=[pltpu.VMEM((32, 128), F32), pltpu.SemaphoreType.DMA((3,))],
+        in_specs=[HBM] * 10,
+        out_specs=(VMEM,) * 11,
+        scratch_shapes=[pltpu.VMEM((32, 128), F32), pltpu.SemaphoreType.DMA((10,))],
         name="coefficients",
         **params(1 << 24),
-    )(level, stays(vectors), stays(leaf_basis), stays(transfer))
-
+    )(
+        stays(vectors),
+        stays(leaf_basis),
+        stays(transfer),
+        stays(far_block),
+        stays(top_block),
+        stays(nearfield_source_leaf.T),
+        stays(near_count),
+        stays(far_source.T),
+        stays(far_count),
+        stays(top_source),
+    )
+
+    outside = lax.ppermute(packed, "leaf", [(n, ((n + 1) ^ 1) - 1) for n in range(1, 63)])
     inside = lax.ppermute(packed, "leaf", [(n, n ^ 1) for n in range(64)])
-    outside = lax.ppermute(packed, "leaf", [(n, ((n + 1) ^ 1) - 1) for n in range(1, 63)])
+    spread = pl.pallas_call(
+        spread_kernel,
+        out_shape=jax.ShapeDtypeStruct((ROOTS // 4, 2 * ROWS, 128), BF),
+        in_specs=[VMEM],
+        out_specs=VMEM,
+        name="spread",
+        **params(1 << 20),
+    )(held(root))
     roots = gathered(spread.reshape(ROOTS // 2, ROWS, 128))
 
     operator = pl.pallas_call(
@@ -331,7 +387,7 @@
             pltpu.VMEM((32, 128), BF),
             pltpu.VMEM((ROWS, 128), jnp.int32),
         ),
-        in_specs=[SMEM] * 2 + [HBM] * 5 + [SMEM] + [VMEM] * 3 + [HBM] * 3 + [VMEM],
+        in_specs=[VMEM] * 8 + [HBM] + [VMEM] * 3,
         out_specs=(VMEM,) * 6,
         scratch_shapes=[
             pltpu.SMEM((4, LEAVES), jnp.int32),
@@ -344,27 +400,22 @@
             pltpu.VMEM((PER_STEP, 32, 128), F32),
             pltpu.VMEM((LEAVES // GROUP, 128, 256), BF),
             pltpu.VMEM((LEAVES, 4, 128, 128), BF),
-            pltpu.VMEM((LEAVES, 4, 1024), BF),
-            pltpu.VMEM((1, 4, 1024), BF),
-            pltpu.SemaphoreType.DMA((STEPS + 7,)),
+            pltpu.SemaphoreType.DMA((STEPS + 5,)),
         ],
         name="near_far",
         **params(1 << 30),
     )(
-        level,
-        leaf,
-        stays(nearfield_source_leaf.T),
-        stays(near_count),
-        stays(far_source.T),
-        stays(far_count),
-        stays(top_source),
-        top_count,
+        held(near_at),
+        held(near_n),
+        held(far_at),
+        held(far_n),
+        held(top_at),
         held(packed),
+        held(outside),
         held(inside),
-        held(outside),
         stays(nearfield_block_matrix),
-        stays(far_block),
-        stays(top_block),
+        held(far),
+        held(top),
         held(basis),
     )
 
@@ -377,11 +428,12 @@
     result = pl.pallas_call(
         final_kernel,
         out_shape=jax.ShapeDtypeStruct((parts, 16, 128), BF),
-        in_specs=[VMEM] * 9,
+        in_specs=[SMEM] + [VMEM] * 9,
         out_specs=VMEM,
         name="final",
         **params(1 << 24),
     )(
+        top_count,
         held(roots),
         held(other_roots),
         held(operator),

time: 32.1 us -> 31.5 us (0.981)
  starting transfers between devices: 20.2 us -> 19.4 us
    ppermute x1, starting transfers between devices: 3.33 us -> 0.09 us  [per_device(): inside = lax.ppermute(packed, 'leaf', [(n, n ^ 1) for n in range(64)])]
    ppermute x1, starting transfers between devices: 1.91 us -> 4.59 us  [per_device(): lax.ppermute(packed, 'leaf', [(n, (n + 1 ^ 1) - 1) for n in range(1, 63)])]
    all_to_all x1, waiting for transfers between devices: 0.26 us -> 1.1 us  [gathered(): lax.all_to_all(spread, 'leaf', 0, 0, tiled=True, axis_index_groups=halves)]
    pallas_call x0 -> x1, Pallas kernels: none -> 0.64 us  [per_device(): pl.pallas_call(spread_kernel, out_shape=jax.ShapeDtypeStruct((ROOTS // 4,...]
    pallas_call x1, Pallas kernels: 2.37 us -> 1.81 us  [per_device(): pl.pallas_call(coef_kernel, out_shape=(pltpu.VMEM((PACKED, 32, 128), BF),...]
    ppermute x1, waiting for transfers between devices: 3.09 us -> 2.55 us  [per_device(): lax.ppermute(roots, 'leaf', [(n, n ^ 6) for n in range(ROOTS)])]
    ppermute x1, starting transfers between devices: 1.3 us -> 0.94 us  [per_device(): lax.ppermute(roots, 'leaf', [(n, n ^ 6) for n in range(ROOTS)])]
  transfers between devices with their start and end apart: 7 -> 7, of which waited for: 2 -> 2; matrix products, arithmetic and copies ran while one was open for 0% -> 0% of each run, Pallas kernels for 12% -> 14%
where the time goes in v4:
time: 31.5 us; the launch traced here: 31.3 us
  starting transfers between devices  19.4 us (62%)
  Pallas kernels  7.46 us (24%)
  waiting for transfers between devices  3.66 us (12%)
  between operations  0.72 us (2%)
    all_to_all x1, starting transfers between devices, gathered(): lax.all_to_all(spread, 'leaf', 0, 0, tiled=True, axis_index_groups=halves)  10.1 us
    ppermute x1, starting transfers between devices, per_device(): lax.ppermute(packed, 'leaf', [(n, (n + 1 ^ 1) - 1) for n in range(1, 63)])  4.59 us
    ppermute x3, starting transfers between devices, per_device(): got[k] = lax.ppermute(out, 'level', [(n, n ^ k) for n in range(4)])  3.69 us
    pallas_call x1, Pallas kernels, per_device(): pl.pallas_call(near_far_kernel, out_shape=(pltpu.VMEM((parts, 16, 128), F...  3.5 us
    ppermute x1, waiting for transfers between devices, per_device(): lax.ppermute(roots, 'leaf', [(n, n ^ 6) for n in range(ROOTS)])  2.55 us
    pallas_call x1, Pallas kernels, per_device(): pl.pallas_call(coef_kernel, out_shape=(pltpu.VMEM((PACKED, 32, 128), BF),...  1.81 us
    pallas_call x1, Pallas kernels, per_device(): pl.pallas_call(final_kernel, out_shape=jax.ShapeDtypeStruct((parts, 16, 1...  1.29 us
    all_to_all x1, waiting for transfers between devices, gathered(): lax.all_to_all(spread, 'leaf', 0, 0, tiled=True, axis_index_groups=halves)  1.1 us
  transfers between devices with their start and end apart: 7, of which 2 were waited for; matrix products, arithmetic and copies ran while one was open for 0% of the time, Pallas kernels for 14%

profile of v4, /device:TPU:1, one launch (start us, length us, event | category | flops | bytes accessed | tf_op | source)
XLA Modules:
  0.0 31.3 jit_solution(2523377321380656363)
XLA Ops:
  0.0 1.8 %coefficients.1 = (bf16[40,32,128]{2,1,0:T(8,128)(2,1)S(1)}, bf16[32,32,128]{2,1,0:T(8,128)(2,1)S(1)}, bf16[32,32,32]{2,1,0:T(8,128)(2,1)S(1)}, bf16[16,128]{1,0...) custom-call(bf16[32,32,128]{2,1,0:T(8,128)(2,1)} %vectors.1, ...), custom_call_target="tpu_custom_call" | custom-call | flops 16777216 | bytes 1048576 | tf_op jit(solution)/shard_map/coefficients/pallas_call | solution.py:324
  1.8 4.6 %collective-permute-start.1 = (bf16[40,32,128]{2,1,0:T(8,128)(2,1)S(1)}, bf16[40,32,128]{2,1,0:T(8,128)(2,1)S(1)}, u32[]{:S(2)}, u32[]{:S(2)}) collective-permute-start(bf16[40,32,128]{2,1,0:T(8,128)(2,1)S(1)} %get-tuple-element.30.own), channel_id=1, source_target_pairs={{4,8},{8,4},{12,16},{16,12},{20,24},{24,20},{28,32},{32,28},{36,40... | collective-permute-start | bytes 983048 | tf_op jit(solution)/shard_map/ppermute | solution.py:357
  6.4 0.1 collective-permute-start.2
  6.5 0.6 %spread.1 = bf16[16,16,128]{2,1,0:T(8,128)(2,1)} custom-call(bf16[16,128]{1,0:T(8,128)(2,1)S(1)} %get-tuple-element.22.root), custom_call_target="tpu_custom_call" | custom-call | flops 1048576 | bytes 1048576 | tf_op jit(solution)/shard_map/spread/pallas_call | solution.py:359
  7.2 10.1 %all-to-all-start = ((bf16[32,8,128]{2,1,0:T(8,128)(2,1)}), bf16[32,8,128]{2,1,0:T(8,128)(2,1)S(1)}, u32[]{:S(2)}, u32[]{:S(2)}) async-start(bf16[32,8,128]{2,1,0:T(8,128)(2,1)} %bitcast.2), calls=%async_computation | async-start | bytes 131072 | tf_op jit(solution)/shard_map/all_to_all | solution.py:303
  17.3 0.0 collective-permute-done.1.outside
  17.3 0.0 collective-permute-done.2.inside
  17.3 3.5 %near_far.1 = (f32[16,16,128]{2,1,0:T(8,128)S(1)}, bf16[19,16,128]{2,1,0:T(8,128)(2,1)S(1)}, bf16[19,16,128]{2,1,0:T(8,128)(2,1)S(1)}, bf16[19,16,128]{2,1,0:T(8...) custom-call(s32[4,32]{1,0:T(4,128)S(1)} %get-tuple-element.25.near_source_in, ...), custom_call_target="tpu_custom_call" | custom-call | flops 1073741824 | bytes 1048576 | tf_op jit(solution)/shard_map/near_far/pallas_call | solution.py:380
  20.8 2.8 %collective-permute-start.3 = (bf16[19,16,128]{2,1,0:T(8,128)(2,1)S(1)}, bf16[19,16,128]{2,1,0:T(8,128)(2,1)S(1)}, u32[]{:S(2)}, u32[]{:S(2)}) collective-permute-start(bf16[19,16,128]{2,1,0:T(8,128)(2,1)S(1)} %get-tuple-element.36), channel_id=1, source_target_pairs={{0,2},{1,3},{2,0},{3,1},{4,6},{5,7},{6,4},{7,5},{8,10},{9,11},{10,... | collective-permute-start | bytes 233480 | tf_op jit(solution)/shard_map/ppermute | solution.py:424
  23.7 0.3 %collective-permute-start.4 = (bf16[19,16,128]{2,1,0:T(8,128)(2,1)S(1)}, bf16[19,16,128]{2,1,0:T(8,128)(2,1)S(1)}, u32[]{:S(2)}, u32[]{:S(2)}) collective-permute-start(bf16[19,16,128]{2,1,0:T(8,128)(2,1)S(1)} %get-tuple-element.37), channel_id=1, source_target_pairs={{0,1},{1,0},{2,3},{3,2},{4,5},{5,4},{6,7},{7,6},{8,9},{9,8},{10,11... | collective-permute-start | bytes 233480 | tf_op jit(solution)/shard_map/ppermute | solution.py:424
  24.0 0.5 %collective-permute-start.5 = (bf16[19,16,128]{2,1,0:T(8,128)(2,1)S(1)}, bf16[19,16,128]{2,1,0:T(8,128)(2,1)S(1)}, u32[]{:S(2)}, u32[]{:S(2)}) collective-permute-start(bf16[19,16,128]{2,1,0:T(8,128)(2,1)S(1)} %get-tuple-element.38), channel_id=1, source_target_pairs={{0,3},{1,2},{2,1},{3,0},{4,7},{5,6},{6,5},{7,4},{8,11},{9,10},{10,... | collective-permute-start | bytes 233480 | tf_op jit(solution)/shard_map/ppermute | solution.py:424
  24.5 1.1 %all-to-all-done.roots = bf16[32,8,128]{2,1,0:T(8,128)(2,1)S(1)} async-done(((bf16[32,8,128]{2,1,0:T(8,128)(2,1)}), bf16[32,8,128]{2,1,0:T(8,128)(2,1)S(1)}, u32[]{:S(2)}, u32[]{:S(2)}) %all-to-all-start) | async-done | bytes 65568 | tf_op jit(solution)/shard_map/all_to_all | solution.py:303
  25.6 0.9 %collective-permute-start = (bf16[32,8,128]{2,1,0:T(8,128)(2,1)S(1)}, bf16[32,8,128]{2,1,0:T(8,128)(2,1)S(1)}, u32[]{:S(2)}, u32[]{:S(2)}) collective-permute-start(bf16[32,8,128]{2,1,0:T(8,128)(2,1)S(1)} %all-to-all-done.roots), channel_id=1, source_target_pairs={{0,24},{4,28},{8,16},{12,20},{16,8},{20,12},{24,0},{28,4},{32,56},... | collective-permute-start | bytes 196616 | tf_op jit(solution)/shard_map/ppermute | solution.py:426
  27.2 0.2 top_operator.1.operator
  27.4 2.5 %collective-permute-done.other_roots = bf16[32,8,128]{2,1,0:T(8,128)(2,1)S(1)} collective-permute-done((bf16[32,8,128]{2,1,0:T(8,128)(2,1)S(1)}, bf16[32,8,128]{2,1,0:T(8,128)(2,1)S(1)}, u32[]{:S(2)}, u32[]{:S(2)}) %collective-permute-start) | collective-permute-done | bytes 65568 | tf_op jit(solution)/shard_map/ppermute | solution.py:426
  30.0 0.0 collective-permute-done.3.got2
  30.0 0.0 collective-permute-done.4.got1
  30.0 0.0 collective-permute-done.5.got3
  30.0 1.3 %final.1 = bf16[16,16,128]{2,1,0:T(8,128)(2,1)} custom-call(s32[1]{0:T(128)S(6)} %copy.13.top_count, bf16[32,8,128]{2,1,0:T(8,128)(2,1)S(1)} %all-to-all-done.roots, bf16[32,8,128]{2,1,0:T(8,128)(2,1)S(1)} %collective-permute-done.other_roots, bf16[64,4096]{1,0:T(8,128)(2,1)S(1)} %top_operator.1.operator, f32[16,16,128]{2,1,0:T(8,128)S(1)} %get-tuple-element.33.kept, ...), custom_call_target="tpu_custom_call" | custom-call | flops 16777216 | bytes 1048576 | tf_op jit(solution)/shard_map/final/pallas_call | solution.py:428
Async XLA Ops:
  1.8 15.5 %collective-permute-start.1 = (bf16[40,32,128]{2,1,0:T(8,128)(2,1)S(1)}, bf16[40,32,128]{2,1,0:T(8,128)(2,1)S(1)}, u32[]{:S(2)}, u32[]{:S(2)}) collective-permute-start(bf16[40,32,128]{2,1,0:T(8,128)(2,1)S(1)} %get-tuple-element.30.own), channel_id=1, source_target_pairs={{4,8},{8,4},{12,16},{16,12},{20,24},{24,20},{28,32},{32,28},{36,40... | collective-permute-start | bytes 983048 | tf_op jit(solution)/shard_map/ppermute | solution.py:357
  6.4 10.9 %collective-permute-start.2 = (bf16[40,32,128]{2,1,0:T(8,128)(2,1)S(1)}, bf16[40,32,128]{2,1,0:T(8,128)(2,1)S(1)}, u32[]{:S(2)}, u32[]{:S(2)}) collective-permute-start(bf16[40,32,128]{2,1,0:T(8,128)(2,1)S(1)} %get-tuple-element.30.own), channel_id=1, source_target_pairs={{0,4},{4,0},{8,12},{12,8},{16,20},{20,16},{24,28},{28,24},{32,36},... | collective-permute-start | bytes 983048 | tf_op jit(solution)/shard_map/ppermute | solution.py:358
  7.2 18.5 %all-to-all-start = ((bf16[32,8,128]{2,1,0:T(8,128)(2,1)}), bf16[32,8,128]{2,1,0:T(8,128)(2,1)S(1)}, u32[]{:S(2)}, u32[]{:S(2)}) async-start(bf16[32,8,128]{2,1,0:T(8,128)(2,1)} %bitcast.2), calls=%async_computation | async-start | bytes 131072 | tf_op jit(solution)/shard_map/all_to_all | solution.py:303
  20.8 9.2 %collective-permute-start.3 = (bf16[19,16,128]{2,1,0:T(8,128)(2,1)S(1)}, bf16[19,16,128]{2,1,0:T(8,128)(2,1)S(1)}, u32[]{:S(2)}, u32[]{:S(2)}) collective-permute-start(bf16[19,16,128]{2,1,0:T(8,128)(2,1)S(1)} %get-tuple-element.36), channel_id=1, source_target_pairs={{0,2},{1,3},{2,0},{3,1},{4,6},{5,7},{6,4},{7,5},{8,10},{9,11},{10,... | collective-permute-start | bytes 233480 | tf_op jit(solution)/shard_map/ppermute | solution.py:424
  23.7 6.3 %collective-permute-start.4 = (bf16[19,16,128]{2,1,0:T(8,128)(2,1)S(1)}, bf16[19,16,128]{2,1,0:T(8,128)(2,1)S(1)}, u32[]{:S(2)}, u32[]{:S(2)}) collective-permute-start(bf16[19,16,128]{2,1,0:T(8,128)(2,1)S(1)} %get-tuple-element.37), channel_id=1, source_target_pairs={{0,1},{1,0},{2,3},{3,2},{4,5},{5,4},{6,7},{7,6},{8,9},{9,8},{10,11... | collective-permute-start | bytes 233480 | tf_op jit(solution)/shard_map/ppermute | solution.py:424
  24.0 6.0 %collective-permute-start.5 = (bf16[19,16,128]{2,1,0:T(8,128)(2,1)S(1)}, bf16[19,16,128]{2,1,0:T(8,128)(2,1)S(1)}, u32[]{:S(2)}, u32[]{:S(2)}) collective-permute-start(bf16[19,16,128]{2,1,0:T(8,128)(2,1)S(1)} %get-tuple-element.38), channel_id=1, source_target_pairs={{0,3},{1,2},{2,1},{3,0},{4,7},{5,6},{6,5},{7,4},{8,11},{9,10},{10,... | collective-permute-start | bytes 233480 | tf_op jit(solution)/shard_map/ppermute | solution.py:424
  25.6 4.4 %collective-permute-start = (bf16[32,8,128]{2,1,0:T(8,128)(2,1)S(1)}, bf16[32,8,128]{2,1,0:T(8,128)(2,1)S(1)}, u32[]{:S(2)}, u32[]{:S(2)}) collective-permute-start(bf16[32,8,128]{2,1,0:T(8,128)(2,1)S(1)} %all-to-all-done.roots), channel_id=1, source_target_pairs={{0,24},{4,28},{8,16},{12,20},{16,8},{20,12},{24,0},{28,4},{32,56},... | collective-permute-start | bytes 196616 | tf_op jit(solution)/shard_map/ppermute | solution.py:426

commit v5 on v4

--- a/solution.py
+++ b/solution.py
@@ -354,7 +354,7 @@
         stays(top_source),
     )
 
-    outside = lax.ppermute(packed, "leaf", [(n, ((n + 1) ^ 1) - 1) for n in range(1, 63)])
+    outside = lax.ppermute(packed, "leaf", [(n, (((n + 1) ^ 1) - 1) % ROOTS) for n in range(ROOTS)])
     inside = lax.ppermute(packed, "leaf", [(n, n ^ 1) for n in range(64)])
     spread = pl.pallas_call(
         spread_kernel,

time: 31.5 us -> 29.8 us (0.946)
  starting transfers between devices: 19.4 us -> 17.6 us
    all_to_all x1, starting transfers between devices: 10.1 us -> 3.64 us  [gathered(): lax.all_to_all(spread, 'leaf', 0, 0, tiled=True, axis_index_groups=halves)]
    ppermute x1, starting transfers between devices: 0.09 us -> 6.56 us  [per_device(): inside = lax.ppermute(packed, 'leaf', [(n, n ^ 1) for n in range(64)])]
    ppermute x1, starting transfers between devices: 4.59 us -> 2.77 us  [per_device(): lax.ppermute(packed, 'leaf', [(n, ((n + 1 ^ 1) - 1) % ROOTS) for n in ran...]
  transfers between devices with their start and end apart: 7 -> 7, of which waited for: 2 -> 2; matrix products, arithmetic and copies ran while one was open for 0% -> 0% of each run, Pallas kernels for 14% -> 15%
where the time goes in v5:
time: 29.8 us; the launch traced here: 29.6 us
  starting transfers between devices  17.6 us (59%)
  Pallas kernels  7.46 us (25%)
  waiting for transfers between devices  3.88 us (13%)
  between operations  0.71 us (2%)
    ppermute x1, starting transfers between devices, per_device(): inside = lax.ppermute(packed, 'leaf', [(n, n ^ 1) for n in range(64)])  6.56 us
    ppermute x3, starting transfers between devices, per_device(): got[k] = lax.ppermute(out, 'level', [(n, n ^ k) for n in range(4)])  3.69 us
    all_to_all x1, starting transfers between devices, gathered(): lax.all_to_all(spread, 'leaf', 0, 0, tiled=True, axis_index_groups=halves)  3.64 us
    pallas_call x1, Pallas kernels, per_device(): pl.pallas_call(near_far_kernel, out_shape=(pltpu.VMEM((parts, 16, 128), F...  3.5 us
    ppermute x1, waiting for transfers between devices, per_device(): lax.ppermute(roots, 'leaf', [(n, n ^ 6) for n in range(ROOTS)])  2.82 us
    ppermute x1, starting transfers between devices, per_device(): lax.ppermute(packed, 'leaf', [(n, ((n + 1 ^ 1) - 1) % ROOTS) for n in ran...  2.77 us
    pallas_call x1, Pallas kernels, per_device(): pl.pallas_call(coef_kernel, out_shape=(pltpu.VMEM((PACKED, 32, 128), BF),...  1.81 us
    pallas_call x1, Pallas kernels, per_device(): pl.pallas_call(final_kernel, out_shape=jax.ShapeDtypeStruct((parts, 16, 1...  1.29 us
  transfers between devices with their start and end apart: 7, of which 2 were waited for; matrix products, arithmetic and copies ran while one was open for 0% of the time, Pallas kernels for 15%

profile of v5, /device:TPU:1, one launch (start us, length us, event | category | flops | bytes accessed | tf_op | source)
XLA Modules:
  0.0 29.6 jit_solution(7483857419142447132)
XLA Ops:
  0.0 1.8 %coefficients.1 = (bf16[40,32,128]{2,1,0:T(8,128)(2,1)S(1)}, bf16[32,32,128]{2,1,0:T(8,128)(2,1)S(1)}, bf16[32,32,32]{2,1,0:T(8,128)(2,1)S(1)}, bf16[16,128]{1,0...) custom-call(bf16[32,32,128]{2,1,0:T(8,128)(2,1)} %vectors.1, ...), custom_call_target="tpu_custom_call" | custom-call | flops 16777216 | bytes 1048576 | tf_op jit(solution)/shard_map/coefficients/pallas_call | solution.py:324
  1.8 2.8 %collective-permute-start.1 = (bf16[40,32,128]{2,1,0:T(8,128)(2,1)S(1)}, bf16[40,32,128]{2,1,0:T(8,128)(2,1)S(1)}, u32[]{:S(2)}, u32[]{:S(2)}) collective-permute-start(bf16[40,32,128]{2,1,0:T(8,128)(2,1)S(1)} %get-tuple-element.30.own), channel_id=1, source_target_pairs={{0,252},{4,8},{8,4},{12,16},{16,12},{20,24},{24,20},{28,32},{32,28... | collective-permute-start | bytes 983048 | tf_op jit(solution)/shard_map/ppermute | solution.py:357
  4.6 6.6 %collective-permute-start.2 = (bf16[40,32,128]{2,1,0:T(8,128)(2,1)S(1)}, bf16[40,32,128]{2,1,0:T(8,128)(2,1)S(1)}, u32[]{:S(2)}, u32[]{:S(2)}) collective-permute-start(bf16[40,32,128]{2,1,0:T(8,128)(2,1)S(1)} %get-tuple-element.30.own), channel_id=1, source_target_pairs={{0,4},{4,0},{8,12},{12,8},{16,20},{20,16},{24,28},{28,24},{32,36},... | collective-permute-start | bytes 983048 | tf_op jit(solution)/shard_map/ppermute | solution.py:358
  11.2 0.6 %spread.1 = bf16[16,16,128]{2,1,0:T(8,128)(2,1)} custom-call(bf16[16,128]{1,0:T(8,128)(2,1)S(1)} %get-tuple-element.22.root), custom_call_target="tpu_custom_call" | custom-call | flops 1048576 | bytes 1048576 | tf_op jit(solution)/shard_map/spread/pallas_call | solution.py:359
  11.8 3.6 %all-to-all-start = ((bf16[32,8,128]{2,1,0:T(8,128)(2,1)}), bf16[32,8,128]{2,1,0:T(8,128)(2,1)S(1)}, u32[]{:S(2)}, u32[]{:S(2)}) async-start(bf16[32,8,128]{2,1,0:T(8,128)(2,1)} %bitcast.2), calls=%async_computation | async-start | bytes 131072 | tf_op jit(solution)/shard_map/all_to_all | solution.py:303
  15.4 0.0 collective-permute-done.1.outside
  15.5 0.0 collective-permute-done.2.inside
  15.5 3.5 %near_far.1 = (f32[16,16,128]{2,1,0:T(8,128)S(1)}, bf16[19,16,128]{2,1,0:T(8,128)(2,1)S(1)}, bf16[19,16,128]{2,1,0:T(8,128)(2,1)S(1)}, bf16[19,16,128]{2,1,0:T(8...) custom-call(s32[4,32]{1,0:T(4,128)S(1)} %get-tuple-element.25.near_source_in, ...), custom_call_target="tpu_custom_call" | custom-call | flops 1073741824 | bytes 1048576 | tf_op jit(solution)/shard_map/near_far/pallas_call | solution.py:380
  19.0 2.8 %collective-permute-start.3 = (bf16[19,16,128]{2,1,0:T(8,128)(2,1)S(1)}, bf16[19,16,128]{2,1,0:T(8,128)(2,1)S(1)}, u32[]{:S(2)}, u32[]{:S(2)}) collective-permute-start(bf16[19,16,128]{2,1,0:T(8,128)(2,1)S(1)} %get-tuple-element.36), channel_id=1, source_target_pairs={{0,2},{1,3},{2,0},{3,1},{4,6},{5,7},{6,4},{7,5},{8,10},{9,11},{10,... | collective-permute-start | bytes 233480 | tf_op jit(solution)/shard_map/ppermute | solution.py:424
  21.8 0.3 %collective-permute-start.4 = (bf16[19,16,128]{2,1,0:T(8,128)(2,1)S(1)}, bf16[19,16,128]{2,1,0:T(8,128)(2,1)S(1)}, u32[]{:S(2)}, u32[]{:S(2)}) collective-permute-start(bf16[19,16,128]{2,1,0:T(8,128)(2,1)S(1)} %get-tuple-element.37), channel_id=1, source_target_pairs={{0,1},{1,0},{2,3},{3,2},{4,5},{5,4},{6,7},{7,6},{8,9},{9,8},{10,11... | collective-permute-start | bytes 233480 | tf_op jit(solution)/shard_map/ppermute | solution.py:424
  22.1 0.5 %collective-permute-start.5 = (bf16[19,16,128]{2,1,0:T(8,128)(2,1)S(1)}, bf16[19,16,128]{2,1,0:T(8,128)(2,1)S(1)}, u32[]{:S(2)}, u32[]{:S(2)}) collective-permute-start(bf16[19,16,128]{2,1,0:T(8,128)(2,1)S(1)} %get-tuple-element.38), channel_id=1, source_target_pairs={{0,3},{1,2},{2,1},{3,0},{4,7},{5,6},{6,5},{7,4},{8,11},{9,10},{10,... | collective-permute-start | bytes 233480 | tf_op jit(solution)/shard_map/ppermute | solution.py:424
  22.7 1.1 %all-to-all-done.roots = bf16[32,8,128]{2,1,0:T(8,128)(2,1)S(1)} async-done(((bf16[32,8,128]{2,1,0:T(8,128)(2,1)}), bf16[32,8,128]{2,1,0:T(8,128)(2,1)S(1)}, u32[]{:S(2)}, u32[]{:S(2)}) %all-to-all-start) | async-done | bytes 65568 | tf_op jit(solution)/shard_map/all_to_all | solution.py:303
  23.7 0.9 %collective-permute-start = (bf16[32,8,128]{2,1,0:T(8,128)(2,1)S(1)}, bf16[32,8,128]{2,1,0:T(8,128)(2,1)S(1)}, u32[]{:S(2)}, u32[]{:S(2)}) collective-permute-start(bf16[32,8,128]{2,1,0:T(8,128)(2,1)S(1)} %all-to-all-done.roots), channel_id=1, source_target_pairs={{0,24},{4,28},{8,16},{12,20},{16,8},{20,12},{24,0},{28,4},{32,56},... | collective-permute-start | bytes 196616 | tf_op jit(solution)/shard_map/ppermute | solution.py:426
  25.3 0.2 top_operator.1.operator
  25.5 2.8 %collective-permute-done.other_roots = bf16[32,8,128]{2,1,0:T(8,128)(2,1)S(1)} collective-permute-done((bf16[32,8,128]{2,1,0:T(8,128)(2,1)S(1)}, bf16[32,8,128]{2,1,0:T(8,128)(2,1)S(1)}, u32[]{:S(2)}, u32[]{:S(2)}) %collective-permute-start) | collective-permute-done | bytes 65568 | tf_op jit(solution)/shard_map/ppermute | solution.py:426
  28.3 0.0 collective-permute-done.3.got2
  28.3 0.0 collective-permute-done.4.got1
  28.3 0.0 collective-permute-done.5.got3
  28.4 1.3 %final.1 = bf16[16,16,128]{2,1,0:T(8,128)(2,1)} custom-call(s32[1]{0:T(128)S(6)} %copy.13.top_count, bf16[32,8,128]{2,1,0:T(8,128)(2,1)S(1)} %all-to-all-done.roots, bf16[32,8,128]{2,1,0:T(8,128)(2,1)S(1)} %collective-permute-done.other_roots, bf16[64,4096]{1,0:T(8,128)(2,1)S(1)} %top_operator.1.operator, f32[16,16,128]{2,1,0:T(8,128)S(1)} %get-tuple-element.33.kept, ...), custom_call_target="tpu_custom_call" | custom-call | flops 16777216 | bytes 1048576 | tf_op jit(solution)/shard_map/final/pallas_call | solution.py:428
Async XLA Ops:
  1.8 13.6 %collective-permute-start.1 = (bf16[40,32,128]{2,1,0:T(8,128)(2,1)S(1)}, bf16[40,32,128]{2,1,0:T(8,128)(2,1)S(1)}, u32[]{:S(2)}, u32[]{:S(2)}) collective-permute-start(bf16[40,32,128]{2,1,0:T(8,128)(2,1)S(1)} %get-tuple-element.30.own), channel_id=1, source_target_pairs={{0,252},{4,8},{8,4},{12,16},{16,12},{20,24},{24,20},{28,32},{32,28... | collective-permute-start | bytes 983048 | tf_op jit(solution)/shard_map/ppermute | solution.py:357
  4.6 10.9 %collective-permute-start.2 = (bf16[40,32,128]{2,1,0:T(8,128)(2,1)S(1)}, bf16[40,32,128]{2,1,0:T(8,128)(2,1)S(1)}, u32[]{:S(2)}, u32[]{:S(2)}) collective-permute-start(bf16[40,32,128]{2,1,0:T(8,128)(2,1)S(1)} %get-tuple-element.30.own), channel_id=1, source_target_pairs={{0,4},{4,0},{8,12},{12,8},{16,20},{20,16},{24,28},{28,24},{32,36},... | collective-permute-start | bytes 983048 | tf_op jit(solution)/shard_map/ppermute | solution.py:358
  11.8 11.9 %all-to-all-start = ((bf16[32,8,128]{2,1,0:T(8,128)(2,1)}), bf16[32,8,128]{2,1,0:T(8,128)(2,1)S(1)}, u32[]{:S(2)}, u32[]{:S(2)}) async-start(bf16[32,8,128]{2,1,0:T(8,128)(2,1)} %bitcast.2), calls=%async_computation | async-start | bytes 131072 | tf_op jit(solution)/shard_map/all_to_all | solution.py:303
  19.0 9.4 %collective-permute-start.3 = (bf16[19,16,128]{2,1,0:T(8,128)(2,1)S(1)}, bf16[19,16,128]{2,1,0:T(8,128)(2,1)S(1)}, u32[]{:S(2)}, u32[]{:S(2)}) collective-permute-start(bf16[19,16,128]{2,1,0:T(8,128)(2,1)S(1)} %get-tuple-element.36), channel_id=1, source_target_pairs={{0,2},{1,3},{2,0},{3,1},{4,6},{5,7},{6,4},{7,5},{8,10},{9,11},{10,... | collective-permute-start | bytes 233480 | tf_op jit(solution)/shard_map/ppermute | solution.py:424
  21.8 6.5 %collective-permute-start.4 = (bf16[19,16,128]{2,1,0:T(8,128)(2,1)S(1)}, bf16[19,16,128]{2,1,0:T(8,128)(2,1)S(1)}, u32[]{:S(2)}, u32[]{:S(2)}) collective-permute-start(bf16[19,16,128]{2,1,0:T(8,128)(2,1)S(1)} %get-tuple-element.37), channel_id=1, source_target_pairs={{0,1},{1,0},{2,3},{3,2},{4,5},{5,4},{6,7},{7,6},{8,9},{9,8},{10,11... | collective-permute-start | bytes 233480 | tf_op jit(solution)/shard_map/ppermute | solution.py:424
  22.1 6.2 %collective-permute-start.5 = (bf16[19,16,128]{2,1,0:T(8,128)(2,1)S(1)}, bf16[19,16,128]{2,1,0:T(8,128)(2,1)S(1)}, u32[]{:S(2)}, u32[]{:S(2)}) collective-permute-start(bf16[19,16,128]{2,1,0:T(8,128)(2,1)S(1)} %get-tuple-element.38), channel_id=1, source_target_pairs={{0,3},{1,2},{2,1},{3,0},{4,7},{5,6},{6,5},{7,4},{8,11},{9,10},{10,... | collective-permute-start | bytes 233480 | tf_op jit(solution)/shard_map/ppermute | solution.py:424
  23.7 4.6 %collective-permute-start = (bf16[32,8,128]{2,1,0:T(8,128)(2,1)S(1)}, bf16[32,8,128]{2,1,0:T(8,128)(2,1)S(1)}, u32[]{:S(2)}, u32[]{:S(2)}) collective-permute-start(bf16[32,8,128]{2,1,0:T(8,128)(2,1)S(1)} %all-to-all-done.roots), channel_id=1, source_target_pairs={{0,24},{4,28},{8,16},{12,20},{16,8},{20,12},{24,0},{28,4},{32,56},... | collective-permute-start | bytes 196616 | tf_op jit(solution)/shard_map/ppermute | solution.py:426

commit v6 on v5

--- a/solution.py
+++ b/solution.py
@@ -15,6 +15,11 @@
 STEPS = 2
 PER_STEP = LEAVES // STEPS
 AHEAD = 2
+OUTSIDE = [
+    (4 * n + k, 4 * n + (k ^ 1) if n in (0, ROOTS - 1) else 4 * (((n + 1) ^ 1) - 1) + k)
+    for n in range(ROOTS)
+    for k in range(4)
+]
 NONE = 3 * LEAVES
 
 
@@ -245,6 +250,18 @@
         operator[32:64, i * 128 : (i + 1) * 128] = low
 
 
+def pack_kernel(roots, after, out):
+    lane = lax.broadcasted_iota(jnp.int32, (ROWS, 128), 1) // 32
+    for n in range(ROOTS // 16):
+        halves = []
+        for h in range(2):
+            v = roots[8 * n + 4 * h].astype(F32)
+            for m in range(1, GROUP):
+                v = jnp.where(lane == m, roots[8 * n + 4 * h + m].astype(F32), v)
+            halves.append(v)
+        out[n] = jnp.concatenate(halves, axis=0).astype(BF)
+
+
 def final_kernel(top_count, roots, other_roots, operator, kept, top_own, names_own, got2, got1, got3, out):
     others = (got1, got2, got3)
     me = lax.axis_index("level")
@@ -260,7 +277,9 @@
         for s in range(4):
             spot = jnp.max(tiles[k][s : s + 1]).astype(jnp.int32)
             index = spot % (ROOTS // 2)
-            tile = jnp.where(spot < ROOTS // 2, roots[index].astype(F32), other_roots[index].astype(F32))
+            tile = jnp.where(spot < ROOTS // 2, roots[index // 8].astype(F32), other_roots[index // 8].astype(F32))
+            tile = jnp.where(index % 8 < 4, tile[0:ROWS], tile[ROWS : 2 * ROWS])
+            tile = pltpu.roll(tile, (s + 4 - index % 4) % 4 * 32, 1)
             live = (me ^ k) * 4 + s < top_count[0]
             c = jnp.where((lane == s) & live, tile, c)
         c = c.astype(BF)
@@ -354,7 +373,7 @@
         stays(top_source),
     )
 
-    outside = lax.ppermute(packed, "leaf", [(n, (((n + 1) ^ 1) - 1) % ROOTS) for n in range(ROOTS)])
+    outside = lax.ppermute(packed, ("leaf", "level"), OUTSIDE)
     inside = lax.ppermute(packed, "leaf", [(n, n ^ 1) for n in range(64)])
     spread = pl.pallas_call(
         spread_kernel,
@@ -423,6 +442,14 @@
     for k, out in ((2, out2), (1, out1), (3, out3)):
         got[k] = lax.ppermute(out, "level", [(n, n ^ k) for n in range(4)])
 
+    roots = pl.pallas_call(
+        pack_kernel,
+        out_shape=pltpu.VMEM((ROOTS // 16, 2 * ROWS, 128), BF),
+        in_specs=[VMEM] * 2,
+        out_specs=VMEM,
+        name="pack",
+        **params(1 << 20),
+    )(held(roots), held(names_own))
     other_roots = lax.ppermute(roots, "leaf", [(n, n ^ 6) for n in range(ROOTS)])
 
     result = pl.pallas_call(

time: 29.8 us -> 29.6 us (level)
  waiting for transfers between devices: 3.88 us -> 3.39 us
    ppermute x1, starting transfers between devices: 6.56 us -> 0.65 us  [per_device(): inside = lax.ppermute(packed, 'leaf', [(n, n ^ 1) for n in range(64)])]
    all_to_all x1, starting transfers between devices: 3.64 us -> 9.49 us  [gathered(): lax.all_to_all(spread, 'leaf', 0, 0, tiled=True, axis_index_groups=halves)]
    ppermute x1, waiting for transfers between devices: 2.82 us -> 2.27 us  [per_device(): lax.ppermute(roots, 'leaf', [(n, n ^ 6) for n in range(ROOTS)])]
where the time goes in v6:
time: 29.6 us; the launch traced here: 29.4 us
  starting transfers between devices  17.6 us (59%)
  Pallas kernels  7.69 us (26%)
  waiting for transfers between devices  3.39 us (11%)
  between operations  0.71 us (2%)
    all_to_all x1, starting transfers between devices, gathered(): lax.all_to_all(spread, 'leaf', 0, 0, tiled=True, axis_index_groups=halves)  9.49 us
    ppermute x3, starting transfers between devices, per_device(): got[k] = lax.ppermute(out, 'level', [(n, n ^ k) for n in range(4)])  3.68 us
    pallas_call x1, Pallas kernels, per_device(): pl.pallas_call(near_far_kernel, out_shape=(pltpu.VMEM((parts, 16, 128), F...  3.51 us
    ppermute x1, starting transfers between devices, per_device(): outside = lax.ppermute(packed, ('leaf', 'level'), OUTSIDE)  2.77 us
    ppermute x1, waiting for transfers between devices, per_device(): lax.ppermute(roots, 'leaf', [(n, n ^ 6) for n in range(ROOTS)])  2.27 us
    pallas_call x1, Pallas kernels, per_device(): pl.pallas_call(coef_kernel, out_shape=(pltpu.VMEM((PACKED, 32, 128), BF),...  1.81 us
    pallas_call x1, Pallas kernels, per_device(): pl.pallas_call(final_kernel, out_shape=jax.ShapeDtypeStruct((parts, 16, 1...  1.5 us
    all_to_all x1, waiting for transfers between devices, gathered(): lax.all_to_all(spread, 'leaf', 0, 0, tiled=True, axis_index_groups=halves)  1.11 us
  transfers between devices with their start and end apart: 7, of which 2 were waited for; matrix products, arithmetic and copies ran while one was open for 0% of the time, Pallas kernels for 15%

profile of v6, /device:TPU:1, one launch (start us, length us, event | category | flops | bytes accessed | tf_op | source)
XLA Modules:
  0.0 29.4 jit_solution(14353844423082737481)
XLA Ops:
  0.0 1.8 %coefficients.1 = (bf16[40,32,128]{2,1,0:T(8,128)(2,1)S(1)}, bf16[32,32,128]{2,1,0:T(8,128)(2,1)S(1)}, bf16[32,32,32]{2,1,0:T(8,128)(2,1)S(1)}, bf16[16,128]{1,0...) custom-call(bf16[32,32,128]{2,1,0:T(8,128)(2,1)} %vectors.1, ...), custom_call_target="tpu_custom_call" | custom-call | flops 16777216 | bytes 1048576 | tf_op jit(solution)/shard_map/coefficients/pallas_call | solution.py:343
  1.8 2.8 %collective-permute-start = (bf16[40,32,128]{2,1,0:T(8,128)(2,1)S(1)}, bf16[40,32,128]{2,1,0:T(8,128)(2,1)S(1)}, u32[]{:S(2)}, u32[]{:S(2)}) collective-permute-start(bf16[40,32,128]{2,1,0:T(8,128)(2,1)S(1)} %get-tuple-element.28.own), channel_id=1, source_target_pairs={{0,1},{1,0},{2,3},{3,2},{4,8},{5,9},{6,10},{7,11},{8,4},{9,5},{10,... | collective-permute-start | bytes 983048 | tf_op jit(solution)/shard_map/ppermute | solution.py:376
  4.6 0.7 %collective-permute-start.1 = (bf16[40,32,128]{2,1,0:T(8,128)(2,1)S(1)}, bf16[40,32,128]{2,1,0:T(8,128)(2,1)S(1)}, u32[]{:S(2)}, u32[]{:S(2)}) collective-permute-start(bf16[40,32,128]{2,1,0:T(8,128)(2,1)S(1)} %get-tuple-element.28.own), channel_id=1, source_target_pairs={{0,4},{4,0},{8,12},{12,8},{16,20},{20,16},{24,28},{28,24},{32,36},... | collective-permute-start | bytes 983048 | tf_op jit(solution)/shard_map/ppermute | solution.py:377
  5.2 0.6 %spread.1 = bf16[16,16,128]{2,1,0:T(8,128)(2,1)} custom-call(bf16[16,128]{1,0:T(8,128)(2,1)S(1)} %get-tuple-element.22.root), custom_call_target="tpu_custom_call" | custom-call | flops 1048576 | bytes 1048576 | tf_op jit(solution)/shard_map/spread/pallas_call | solution.py:378
  5.9 9.5 %all-to-all-start = ((bf16[32,8,128]{2,1,0:T(8,128)(2,1)}), bf16[32,8,128]{2,1,0:T(8,128)(2,1)S(1)}, u32[]{:S(2)}, u32[]{:S(2)}) async-start(bf16[32,8,128]{2,1,0:T(8,128)(2,1)} %bitcast.2), calls=%async_computation | async-start | bytes 131072 | tf_op jit(solution)/shard_map/all_to_all | solution.py:322
  15.4 0.0 collective-permute-done.outside
  15.4 0.0 collective-permute-done.1.inside
  15.4 3.5 %near_far.1 = (f32[16,16,128]{2,1,0:T(8,128)S(1)}, bf16[19,16,128]{2,1,0:T(8,128)(2,1)S(1)}, bf16[19,16,128]{2,1,0:T(8,128)(2,1)S(1)}, bf16[19,16,128]{2,1,0:T(8...) custom-call(s32[4,32]{1,0:T(4,128)S(1)} %get-tuple-element.23.near_source_in, ...), custom_call_target="tpu_custom_call" | custom-call | flops 1073741824 | bytes 1048576 | tf_op jit(solution)/shard_map/near_far/pallas_call | solution.py:399
  18.9 2.8 %collective-permute-start.3 = (bf16[19,16,128]{2,1,0:T(8,128)(2,1)S(1)}, bf16[19,16,128]{2,1,0:T(8,128)(2,1)S(1)}, u32[]{:S(2)}, u32[]{:S(2)}) collective-permute-start(bf16[19,16,128]{2,1,0:T(8,128)(2,1)S(1)} %get-tuple-element.36), channel_id=1, source_target_pairs={{0,2},{1,3},{2,0},{3,1},{4,6},{5,7},{6,4},{7,5},{8,10},{9,11},{10,... | collective-permute-start | bytes 233480 | tf_op jit(solution)/shard_map/ppermute | solution.py:443
  21.7 0.3 %collective-permute-start.4 = (bf16[19,16,128]{2,1,0:T(8,128)(2,1)S(1)}, bf16[19,16,128]{2,1,0:T(8,128)(2,1)S(1)}, u32[]{:S(2)}, u32[]{:S(2)}) collective-permute-start(bf16[19,16,128]{2,1,0:T(8,128)(2,1)S(1)} %get-tuple-element.37), channel_id=1, source_target_pairs={{0,1},{1,0},{2,3},{3,2},{4,5},{5,4},{6,7},{7,6},{8,9},{9,8},{10,11... | collective-permute-start | bytes 233480 | tf_op jit(solution)/shard_map/ppermute | solution.py:443
  22.1 0.5 %collective-permute-start.5 = (bf16[19,16,128]{2,1,0:T(8,128)(2,1)S(1)}, bf16[19,16,128]{2,1,0:T(8,128)(2,1)S(1)}, u32[]{:S(2)}, u32[]{:S(2)}) collective-permute-start(bf16[19,16,128]{2,1,0:T(8,128)(2,1)S(1)} %get-tuple-element.38), channel_id=1, source_target_pairs={{0,3},{1,2},{2,1},{3,0},{4,7},{5,6},{6,5},{7,4},{8,11},{9,10},{10,... | collective-permute-start | bytes 233480 | tf_op jit(solution)/shard_map/ppermute | solution.py:443
  22.6 1.1 %all-to-all-done.roots = bf16[32,8,128]{2,1,0:T(8,128)(2,1)S(1)} async-done(((bf16[32,8,128]{2,1,0:T(8,128)(2,1)}), bf16[32,8,128]{2,1,0:T(8,128)(2,1)S(1)}, u32[]{:S(2)}, u32[]{:S(2)}) %all-to-all-start) | async-done | bytes 65568 | tf_op jit(solution)/shard_map/all_to_all | solution.py:322
  23.7 1.0 %collective-permute-start.2 = (bf16[4,16,128]{2,1,0:T(8,128)(2,1)S(1)}, bf16[4,16,128]{2,1,0:T(8,128)(2,1)S(1)}, u32[]{:S(2)}, u32[]{:S(2)}) collective-permute-start(bf16[4,16,128]{2,1,0:T(8,128)(2,1)S(1)} %pack.1.roots), channel_id=1, source_target_pairs={{0,24},{4,28},{8,16},{12,20},{16,8},{20,12},{24,0},{28,4},{32,56},... | collective-permute-start | bytes 49160 | tf_op jit(solution)/shard_map/ppermute | solution.py:453
  25.4 0.2 top_operator.1.operator
  25.6 2.3 %collective-permute-done.2.other_roots = bf16[4,16,128]{2,1,0:T(8,128)(2,1)S(1)} collective-permute-done((bf16[4,16,128]{2,1,0:T(8,128)(2,1)S(1)}, bf16[4,16,128]{2,1,0:T(8,128)(2,1)S(1)}, u32[]{:S(2)}, u32[]{:S(2)}) %collective-permute-start.2) | collective-permute-done | bytes 16416 | tf_op jit(solution)/shard_map/ppermute | solution.py:453
  27.9 0.0 collective-permute-done.3.got2
  27.9 0.0 collective-permute-done.4.got1
  27.9 0.0 collective-permute-done.5.got3
  27.9 1.5 %final.1 = bf16[16,16,128]{2,1,0:T(8,128)(2,1)} custom-call(s32[1]{0:T(128)S(6)} %copy.13.top_count, bf16[4,16,128]{2,1,0:T(8,128)(2,1)S(1)} %pack.1.roots, bf16[4,16,128]{2,1,0:T(8,128)(2,1)S(1)} %collective-permute-done.2.other_roots, bf16[64,4096]{1,0:T(8,128)(2,1)S(1)} %top_operator.1.operator, f32[16,16,128]{2,1,0:T(8,128)S(1)} %get-tuple-element.34.kept, ...), custom_call_target="tpu_custom_call" | custom-call | flops 16777216 | bytes 1048576 | tf_op jit(solution)/shard_map/final/pallas_call | solution.py:455
  (1 shorter events, 0.0 us)
Async XLA Ops:
  1.8 13.6 %collective-permute-start = (bf16[40,32,128]{2,1,0:T(8,128)(2,1)S(1)}, bf16[40,32,128]{2,1,0:T(8,128)(2,1)S(1)}, u32[]{:S(2)}, u32[]{:S(2)}) collective-permute-start(bf16[40,32,128]{2,1,0:T(8,128)(2,1)S(1)} %get-tuple-element.28.own), channel_id=1, source_target_pairs={{0,1},{1,0},{2,3},{3,2},{4,8},{5,9},{6,10},{7,11},{8,4},{9,5},{10,... | collective-permute-start | bytes 983048 | tf_op jit(solution)/shard_map/ppermute | solution.py:376
  4.6 10.8 %collective-permute-start.1 = (bf16[40,32,128]{2,1,0:T(8,128)(2,1)S(1)}, bf16[40,32,128]{2,1,0:T(8,128)(2,1)S(1)}, u32[]{:S(2)}, u32[]{:S(2)}) collective-permute-start(bf16[40,32,128]{2,1,0:T(8,128)(2,1)S(1)} %get-tuple-element.28.own), channel_id=1, source_target_pairs={{0,4},{4,0},{8,12},{12,8},{16,20},{20,16},{24,28},{28,24},{32,36},... | collective-permute-start | bytes 983048 | tf_op jit(solution)/shard_map/ppermute | solution.py:377
  5.9 17.8 %all-to-all-start = ((bf16[32,8,128]{2,1,0:T(8,128)(2,1)}), bf16[32,8,128]{2,1,0:T(8,128)(2,1)S(1)}, u32[]{:S(2)}, u32[]{:S(2)}) async-start(bf16[32,8,128]{2,1,0:T(8,128)(2,1)} %bitcast.2), calls=%async_computation | async-start | bytes 131072 | tf_op jit(solution)/shard_map/all_to_all | solution.py:322
  18.9 9.0 %collective-permute-start.3 = (bf16[19,16,128]{2,1,0:T(8,128)(2,1)S(1)}, bf16[19,16,128]{2,1,0:T(8,128)(2,1)S(1)}, u32[]{:S(2)}, u32[]{:S(2)}) collective-permute-start(bf16[19,16,128]{2,1,0:T(8,128)(2,1)S(1)} %get-tuple-element.36), channel_id=1, source_target_pairs={{0,2},{1,3},{2,0},{3,1},{4,6},{5,7},{6,4},{7,5},{8,10},{9,11},{10,... | collective-permute-start | bytes 233480 | tf_op jit(solution)/shard_map/ppermute | solution.py:443
  21.7 6.2 %collective-permute-start.4 = (bf16[19,16,128]{2,1,0:T(8,128)(2,1)S(1)}, bf16[19,16,128]{2,1,0:T(8,128)(2,1)S(1)}, u32[]{:S(2)}, u32[]{:S(2)}) collective-permute-start(bf16[19,16,128]{2,1,0:T(8,128)(2,1)S(1)} %get-tuple-element.37), channel_id=1, source_target_pairs={{0,1},{1,0},{2,3},{3,2},{4,5},{5,4},{6,7},{7,6},{8,9},{9,8},{10,11... | collective-permute-start | bytes 233480 | tf_op jit(solution)/shard_map/ppermute | solution.py:443
  22.1 5.8 %collective-permute-start.5 = (bf16[19,16,128]{2,1,0:T(8,128)(2,1)S(1)}, bf16[19,16,128]{2,1,0:T(8,128)(2,1)S(1)}, u32[]{:S(2)}, u32[]{:S(2)}) collective-permute-start(bf16[19,16,128]{2,1,0:T(8,128)(2,1)S(1)} %get-tuple-element.38), channel_id=1, source_target_pairs={{0,3},{1,2},{2,1},{3,0},{4,7},{5,6},{6,5},{7,4},{8,11},{9,10},{10,... | collective-permute-start | bytes 233480 | tf_op jit(solution)/shard_map/ppermute | solution.py:443
  23.7 4.2 %collective-permute-start.2 = (bf16[4,16,128]{2,1,0:T(8,128)(2,1)S(1)}, bf16[4,16,128]{2,1,0:T(8,128)(2,1)S(1)}, u32[]{:S(2)}, u32[]{:S(2)}) collective-permute-start(bf16[4,16,128]{2,1,0:T(8,128)(2,1)S(1)} %pack.1.roots), channel_id=1, source_target_pairs={{0,24},{4,28},{8,16},{12,20},{16,8},{20,12},{24,0},{28,4},{32,56},... | collective-permute-start | bytes 49160 | tf_op jit(solution)/shard_map/ppermute | solution.py:453

commit v7 on v6

--- a/solution.py
+++ b/solution.py
@@ -262,7 +262,7 @@
         out[n] = jnp.concatenate(halves, axis=0).astype(BF)
 
 
-def final_kernel(top_count, roots, other_roots, operator, kept, top_own, names_own, got2, got1, got3, out):
+def final_kernel(top_count, roots, other_roots, operator, kept, top_own, names_own, got2, got3, got1, out):
     others = (got1, got2, got3)
     me = lax.axis_index("level")
     tiles = [names_own[...].astype(F32)]
@@ -439,7 +439,7 @@
     )
 
     got = {}
-    for k, out in ((2, out2), (1, out1), (3, out3)):
+    for k, out in ((2, out2), (3, out3), (1, out1)):
         got[k] = lax.ppermute(out, "level", [(n, n ^ k) for n in range(4)])
 
     roots = pl.pallas_call(
@@ -468,8 +468,8 @@
         held(top_own),
         held(names_own),
         held(got[2]),
+        held(got[3]),
         held(got[1]),
-        held(got[3]),
     )
     return result.reshape(LEAVES, ROWS, 128)
 

time: 29.6 us -> 29.3 us (0.990)
  no operation moved by 1% of the time
where the time goes in v7:
time: 29.3 us; the launch traced here: 29.1 us
  starting transfers between devices  17.6 us (60%)
  Pallas kernels  7.69 us (26%)
  waiting for transfers between devices  3.1 us (11%)
  between operations  0.71 us (2%)
    all_to_all x1, starting transfers between devices, gathered(): lax.all_to_all(spread, 'leaf', 0, 0, tiled=True, axis_index_groups=halves)  9.49 us
    ppermute x3, starting transfers between devices, per_device(): got[k] = lax.ppermute(out, 'level', [(n, n ^ k) for n in range(4)])  3.69 us
    pallas_call x1, Pallas kernels, per_device(): pl.pallas_call(near_far_kernel, out_shape=(pltpu.VMEM((parts, 16, 128), F...  3.5 us
    ppermute x1, starting transfers between devices, per_device(): outside = lax.ppermute(packed, ('leaf', 'level'), OUTSIDE)  2.77 us
    ppermute x1, waiting for transfers between devices, per_device(): lax.ppermute(roots, 'leaf', [(n, n ^ 6) for n in range(ROOTS)])  1.98 us
    pallas_call x1, Pallas kernels, per_device(): pl.pallas_call(coef_kernel, out_shape=(pltpu.VMEM((PACKED, 32, 128), BF),...  1.81 us
    pallas_call x1, Pallas kernels, per_device(): pl.pallas_call(final_kernel, out_shape=jax.ShapeDtypeStruct((parts, 16, 1...  1.5 us
    all_to_all x1, waiting for transfers between devices, gathered(): lax.all_to_all(spread, 'leaf', 0, 0, tiled=True, axis_index_groups=halves)  1.11 us
  transfers between devices with their start and end apart: 7, of which 2 were waited for; matrix products, arithmetic and copies ran while one was open for 0% of the time, Pallas kernels for 15%

profile of v7, /device:TPU:1, one launch (start us, length us, event | category | flops | bytes accessed | tf_op | source)
XLA Modules:
  0.0 29.1 jit_solution(2140101167975153274)
XLA Ops:
  0.0 1.8 %coefficients.1 = (bf16[40,32,128]{2,1,0:T(8,128)(2,1)S(1)}, bf16[32,32,128]{2,1,0:T(8,128)(2,1)S(1)}, bf16[32,32,32]{2,1,0:T(8,128)(2,1)S(1)}, bf16[16,128]{1,0...) custom-call(bf16[32,32,128]{2,1,0:T(8,128)(2,1)} %vectors.1, ...), custom_call_target="tpu_custom_call" | custom-call | flops 16777216 | bytes 1048576 | tf_op jit(solution)/shard_map/coefficients/pallas_call | solution.py:343
  1.8 2.8 %collective-permute-start = (bf16[40,32,128]{2,1,0:T(8,128)(2,1)S(1)}, bf16[40,32,128]{2,1,0:T(8,128)(2,1)S(1)}, u32[]{:S(2)}, u32[]{:S(2)}) collective-permute-start(bf16[40,32,128]{2,1,0:T(8,128)(2,1)S(1)} %get-tuple-element.28.own), channel_id=1, source_target_pairs={{0,1},{1,0},{2,3},{3,2},{4,8},{5,9},{6,10},{7,11},{8,4},{9,5},{10,... | collective-permute-start | bytes 983048 | tf_op jit(solution)/shard_map/ppermute | solution.py:376
  4.6 0.7 %collective-permute-start.1 = (bf16[40,32,128]{2,1,0:T(8,128)(2,1)S(1)}, bf16[40,32,128]{2,1,0:T(8,128)(2,1)S(1)}, u32[]{:S(2)}, u32[]{:S(2)}) collective-permute-start(bf16[40,32,128]{2,1,0:T(8,128)(2,1)S(1)} %get-tuple-element.28.own), channel_id=1, source_target_pairs={{0,4},{4,0},{8,12},{12,8},{16,20},{20,16},{24,28},{28,24},{32,36},... | collective-permute-start | bytes 983048 | tf_op jit(solution)/shard_map/ppermute | solution.py:377
  5.2 0.6 %spread.1 = bf16[16,16,128]{2,1,0:T(8,128)(2,1)} custom-call(bf16[16,128]{1,0:T(8,128)(2,1)S(1)} %get-tuple-element.22.root), custom_call_target="tpu_custom_call" | custom-call | flops 1048576 | bytes 1048576 | tf_op jit(solution)/shard_map/spread/pallas_call | solution.py:378
  5.9 9.5 %all-to-all-start = ((bf16[32,8,128]{2,1,0:T(8,128)(2,1)}), bf16[32,8,128]{2,1,0:T(8,128)(2,1)S(1)}, u32[]{:S(2)}, u32[]{:S(2)}) async-start(bf16[32,8,128]{2,1,0:T(8,128)(2,1)} %bitcast.2), calls=%async_computation | async-start | bytes 131072 | tf_op jit(solution)/shard_map/all_to_all | solution.py:322
  15.4 0.0 collective-permute-done.outside
  15.4 0.0 collective-permute-done.1.inside
  15.4 3.5 %near_far.1 = (f32[16,16,128]{2,1,0:T(8,128)S(1)}, bf16[19,16,128]{2,1,0:T(8,128)(2,1)S(1)}, bf16[19,16,128]{2,1,0:T(8,128)(2,1)S(1)}, bf16[19,16,128]{2,1,0:T(8...) custom-call(s32[4,32]{1,0:T(4,128)S(1)} %get-tuple-element.23.near_source_in, ...), custom_call_target="tpu_custom_call" | custom-call | flops 1073741824 | bytes 1048576 | tf_op jit(solution)/shard_map/near_far/pallas_call | solution.py:399
  18.9 2.8 %collective-permute-start.3 = (bf16[19,16,128]{2,1,0:T(8,128)(2,1)S(1)}, bf16[19,16,128]{2,1,0:T(8,128)(2,1)S(1)}, u32[]{:S(2)}, u32[]{:S(2)}) collective-permute-start(bf16[19,16,128]{2,1,0:T(8,128)(2,1)S(1)} %get-tuple-element.36), channel_id=1, source_target_pairs={{0,2},{1,3},{2,0},{3,1},{4,6},{5,7},{6,4},{7,5},{8,10},{9,11},{10,... | collective-permute-start | bytes 233480 | tf_op jit(solution)/shard_map/ppermute | solution.py:443
  21.7 0.8 %collective-permute-start.4 = (bf16[19,16,128]{2,1,0:T(8,128)(2,1)S(1)}, bf16[19,16,128]{2,1,0:T(8,128)(2,1)S(1)}, u32[]{:S(2)}, u32[]{:S(2)}) collective-permute-start(bf16[19,16,128]{2,1,0:T(8,128)(2,1)S(1)} %get-tuple-element.37), channel_id=1, source_target_pairs={{0,3},{1,2},{2,1},{3,0},{4,7},{5,6},{6,5},{7,4},{8,11},{9,10},{10,... | collective-permute-start | bytes 233480 | tf_op jit(solution)/shard_map/ppermute | solution.py:443
  22.6 0.0 collective-permute-start.5
  22.6 1.1 %all-to-all-done.roots = bf16[32,8,128]{2,1,0:T(8,128)(2,1)S(1)} async-done(((bf16[32,8,128]{2,1,0:T(8,128)(2,1)}), bf16[32,8,128]{2,1,0:T(8,128)(2,1)S(1)}, u32[]{:S(2)}, u32[]{:S(2)}) %all-to-all-start) | async-done | bytes 65568 | tf_op jit(solution)/shard_map/all_to_all | solution.py:322
  23.7 1.0 %collective-permute-start.2 = (bf16[4,16,128]{2,1,0:T(8,128)(2,1)S(1)}, bf16[4,16,128]{2,1,0:T(8,128)(2,1)S(1)}, u32[]{:S(2)}, u32[]{:S(2)}) collective-permute-start(bf16[4,16,128]{2,1,0:T(8,128)(2,1)S(1)} %pack.1.roots), channel_id=1, source_target_pairs={{0,24},{4,28},{8,16},{12,20},{16,8},{20,12},{24,0},{28,4},{32,56},... | collective-permute-start | bytes 49160 | tf_op jit(solution)/shard_map/ppermute | solution.py:453
  25.4 0.2 top_operator.1.operator
  25.6 2.0 %collective-permute-done.2.other_roots = bf16[4,16,128]{2,1,0:T(8,128)(2,1)S(1)} collective-permute-done((bf16[4,16,128]{2,1,0:T(8,128)(2,1)S(1)}, bf16[4,16,128]{2,1,0:T(8,128)(2,1)S(1)}, u32[]{:S(2)}, u32[]{:S(2)}) %collective-permute-start.2) | collective-permute-done | bytes 16416 | tf_op jit(solution)/shard_map/ppermute | solution.py:453
  27.6 0.0 collective-permute-done.3.got2
  27.6 0.0 collective-permute-done.4.got3
  27.6 0.0 collective-permute-done.5.got1
  27.6 1.5 %final.1 = bf16[16,16,128]{2,1,0:T(8,128)(2,1)} custom-call(s32[1]{0:T(128)S(6)} %copy.13.top_count, bf16[4,16,128]{2,1,0:T(8,128)(2,1)S(1)} %pack.1.roots, bf16[4,16,128]{2,1,0:T(8,128)(2,1)S(1)} %collective-permute-done.2.other_roots, bf16[64,4096]{1,0:T(8,128)(2,1)S(1)} %top_operator.1.operator, f32[16,16,128]{2,1,0:T(8,128)S(1)} %get-tuple-element.34.kept, ...), custom_call_target="tpu_custom_call" | custom-call | flops 16777216 | bytes 1048576 | tf_op jit(solution)/shard_map/final/pallas_call | solution.py:455
  (1 shorter events, 0.0 us)
Async XLA Ops:
  1.8 13.6 %collective-permute-start = (bf16[40,32,128]{2,1,0:T(8,128)(2,1)S(1)}, bf16[40,32,128]{2,1,0:T(8,128)(2,1)S(1)}, u32[]{:S(2)}, u32[]{:S(2)}) collective-permute-start(bf16[40,32,128]{2,1,0:T(8,128)(2,1)S(1)} %get-tuple-element.28.own), channel_id=1, source_target_pairs={{0,1},{1,0},{2,3},{3,2},{4,8},{5,9},{6,10},{7,11},{8,4},{9,5},{10,... | collective-permute-start | bytes 983048 | tf_op jit(solution)/shard_map/ppermute | solution.py:376
  4.6 10.8 %collective-permute-start.1 = (bf16[40,32,128]{2,1,0:T(8,128)(2,1)S(1)}, bf16[40,32,128]{2,1,0:T(8,128)(2,1)S(1)}, u32[]{:S(2)}, u32[]{:S(2)}) collective-permute-start(bf16[40,32,128]{2,1,0:T(8,128)(2,1)S(1)} %get-tuple-element.28.own), channel_id=1, source_target_pairs={{0,4},{4,0},{8,12},{12,8},{16,20},{20,16},{24,28},{28,24},{32,36},... | collective-permute-start | bytes 983048 | tf_op jit(solution)/shard_map/ppermute | solution.py:377
  5.9 17.8 %all-to-all-start = ((bf16[32,8,128]{2,1,0:T(8,128)(2,1)}), bf16[32,8,128]{2,1,0:T(8,128)(2,1)S(1)}, u32[]{:S(2)}, u32[]{:S(2)}) async-start(bf16[32,8,128]{2,1,0:T(8,128)(2,1)} %bitcast.2), calls=%async_computation | async-start | bytes 131072 | tf_op jit(solution)/shard_map/all_to_all | solution.py:322
  18.9 8.7 %collective-permute-start.3 = (bf16[19,16,128]{2,1,0:T(8,128)(2,1)S(1)}, bf16[19,16,128]{2,1,0:T(8,128)(2,1)S(1)}, u32[]{:S(2)}, u32[]{:S(2)}) collective-permute-start(bf16[19,16,128]{2,1,0:T(8,128)(2,1)S(1)} %get-tuple-element.36), channel_id=1, source_target_pairs={{0,2},{1,3},{2,0},{3,1},{4,6},{5,7},{6,4},{7,5},{8,10},{9,11},{10,... | collective-permute-start | bytes 233480 | tf_op jit(solution)/shard_map/ppermute | solution.py:443
  21.7 5.9 %collective-permute-start.4 = (bf16[19,16,128]{2,1,0:T(8,128)(2,1)S(1)}, bf16[19,16,128]{2,1,0:T(8,128)(2,1)S(1)}, u32[]{:S(2)}, u32[]{:S(2)}) collective-permute-start(bf16[19,16,128]{2,1,0:T(8,128)(2,1)S(1)} %get-tuple-element.37), channel_id=1, source_target_pairs={{0,3},{1,2},{2,1},{3,0},{4,7},{5,6},{6,5},{7,4},{8,11},{9,10},{10,... | collective-permute-start | bytes 233480 | tf_op jit(solution)/shard_map/ppermute | solution.py:443
  22.6 5.0 %collective-permute-start.5 = (bf16[19,16,128]{2,1,0:T(8,128)(2,1)S(1)}, bf16[19,16,128]{2,1,0:T(8,128)(2,1)S(1)}, u32[]{:S(2)}, u32[]{:S(2)}) collective-permute-start(bf16[19,16,128]{2,1,0:T(8,128)(2,1)S(1)} %get-tuple-element.38), channel_id=1, source_target_pairs={{0,1},{1,0},{2,3},{3,2},{4,5},{5,4},{6,7},{7,6},{8,9},{9,8},{10,11... | collective-permute-start | bytes 233480 | tf_op jit(solution)/shard_map/ppermute | solution.py:443
  23.7 3.9 %collective-permute-start.2 = (bf16[4,16,128]{2,1,0:T(8,128)(2,1)S(1)}, bf16[4,16,128]{2,1,0:T(8,128)(2,1)S(1)}, u32[]{:S(2)}, u32[]{:S(2)}) collective-permute-start(bf16[4,16,128]{2,1,0:T(8,128)(2,1)S(1)} %pack.1.roots), channel_id=1, source_target_pairs={{0,24},{4,28},{8,16},{12,20},{16,8},{20,12},{24,0},{28,4},{32,56},... | collective-permute-start | bytes 49160 | tf_op jit(solution)/shard_map/ppermute | solution.py:453
